TPU v7x, 256 devices: a whole 4x4x8 slice. The times are simulated.
256 devices in a mesh: row: 8 (over y, core), col: 32 (over x, z).
Axes of the slice: x: 4, y: 4, z: 8, core: 2. Of those that a mesh axis runs over, the one named last changes fastest.
Arguments:
- momentum: float32 [8192, 26624], P('row', 'col'), may hold values from -6 to 6
- gradient: bfloat16 [8192, 26624], P('row', 'col'), may hold values from -6 to 6
- right_factor: float32 [26624, 128], P('col'), may hold values from -0.0390625 to 0.0390625
Outputs:
- new_momentum: float32 [8192, 26624], P('row', 'col')
- update: bfloat16 [8192, 26624], P('row', 'col')
All inputs are finite; a program needn't handle non-finite values.
Results may differ from a plain program's by a relative error of at most 0.001.
Values sent between devices are 32-bit elements; how exact they have to be, the bound alone decides.
No kernel may reach another device: no remote copies, remote signals or barrier semaphores. Data moves between devices by JAX's collectives and lax.ppermute only.
A program may use at most 64 MiB of HBM per device.

v0:
```python
import jax
import jax.numpy as jnp
from jax import lax
from jax.sharding import PartitionSpec as P

ROWS = 8192
COLS = 26624
RANK = 128


def contract_first(first, second):
    return lax.dot_general(first, second, (((0,), (0,)), ((), ())), precision=lax.Precision.HIGHEST)


def orthonormal(left, gram):
    lower = jnp.linalg.cholesky(gram)
    return lax.linalg.triangular_solve(lower, left, left_side=False, lower=True, transpose_a=True)


def body(momentum, gradient, right_factor):
    high = lax.Precision.HIGHEST
    blend = momentum + gradient.astype(jnp.float32)
    left = lax.psum(jnp.dot(blend, right_factor, precision=high), "col")
    gram = lax.psum(contract_first(left, left), "row")
    basis = orthonormal(left, gram)
    across = lax.psum(contract_first(blend, basis), "row")
    colsq = lax.psum(jnp.sum(across * across, axis=0), "col")
    fresh = across / jnp.sqrt(colsq + 1e-06)
    new_momentum = blend - 0.05 * jnp.dot(basis, across.T, precision=high)
    scale_factor = (ROWS * COLS / RANK) ** 0.5
    update = (scale_factor * jnp.dot(basis, fresh.T, precision=high)).astype(jnp.bfloat16)
    return (new_momentum, update)


def solution(mesh):
    in_specs = (P("row", "col"), P("row", "col"), P("col", None))
    out_specs = (P("row", "col"), P("row", "col"))
    return jax.shard_map(body, mesh=mesh, in_specs=in_specs, out_specs=out_specs, check_vma=False)
```

profile of v0, /device:TPU:0, one launch (start us, length us, event | category | flops | bytes accessed | tf_op | source)
XLA Modules:
  0.0 420.2 jit_solution(9809215506430784828)
XLA Ops:
  7.2 0.0 all-reduce.4.cloned.1.call-start
  7.2 0.9 copy-done
  8.2 9.7 %fusion.1 = f32[1024,128]{1,0:T(8,128)} fusion(f32[832,128]{1,0:T(8,128)S(1)} %copy-done, f32[1024,832]{0,1:T(8,128)} %param.3, bf16[1024,832]{0,1:T(8,128)(2,1)} %param.4), kind=kOutput, calls=%fused_computation.4 | convolution fusion | flops 1310326784 | bytes 6062080 | tf_op jit(solution)/shard_map/dot_general | solution.py:23
  17.9 0.0 all-reduce.4.cloned.1.call-update
  17.9 0.0 all-reduce.6.cloned.1.call-start
  17.9 148.7 %all-reduce.4.cloned.1.call-done = f32[1024,128]{1,0:T(8,128)} async-done(((f32[1024,128]{1,0:T(8,128)}), f32[1024,128]{1,0:T(8,128)}) %all-reduce.4.cloned.1.call-update) | async-done | bytes 524304 | tf_op jit(solution)/shard_map/psum | solution.py:23
  166.7 2.8 fusion.8
  169.5 0.0 all-reduce.6.cloned.1.call-update
  169.5 0.2 all-reduce.8.cloned.1.call-start
  169.7 60.8 %all-reduce.6.cloned.1.call-done = f32[128,128]{0,1:T(8,128)} async-done(((f32[128,128]{0,1:T(8,128)}), f32[128,128]{0,1:T(8,128)}) %all-reduce.6.cloned.1.call-update) | async-done | bytes 65552 | tf_op jit(solution)/shard_map/psum | solution.py:24
  230.5 0.9 copy.6
  231.4 0.9 fusion.7
  232.3 11.7 %cholesky.16 = f32[128,128]{1,0:T(8,128)S(1)} custom-call(f32[128,128]{1,0:T(8,128)S(1)} %fusion.7), custom_call_target="Cholesky" | custom-call | tf_op jit(solution)/shard_map/jit(cholesky)/cholesky | solution.py:16
  244.0 0.6 compare_reduce_fusion
  244.7 0.7 fusion.4
  245.4 9.8 %custom-call.6 = f32[1,128,128]{1,2,0:T(8,128)S(1)} custom-call(f32[1,128,128]{2,1,0:T(8,128)S(1)} %fusion.4), custom_call_target="InvertDiagBlocksLowerTriangular" | custom-call | tf_op jit(solution)/shard_map/triangular_solve | solution.py:17
  255.2 1.6 fusion.5
  256.8 5.5 %fusion = f32[832,128]{1,0:T(8,128)} fusion(f32[1024,128]{1,0:T(8,128)S(1)} %fusion.5, f32[1024,832]{0,1:T(8,128)} %param.3, bf16[1024,832]{0,1:T(8,128)(2,1)S(1)} %copy-done.1), kind=kOutput, calls=%fused_computation.3 | convolution fusion | flops 1310326784 | bytes 6062080 | tf_op jit(solution)/shard_map/dot_general | solution.py:12
  262.3 0.0 all-reduce.8.cloned.1.call-update
  262.3 64.9 %all-reduce.8.cloned.1.call-done = f32[832,128]{1,0:T(8,128)} async-done(((f32[832,128]{1,0:T(8,128)}), f32[832,128]{1,0:T(8,128)}) %all-reduce.8.cloned.1.call-update) | async-done | bytes 426000 | tf_op jit(solution)/shard_map/psum | solution.py:26
  327.2 1.1 multiply_reduce_fusion
  328.4 75.3 %psum.31 = f32[128]{0:T(128)S(1)} all-reduce(f32[128]{0:T(128)S(1)} %multiply_reduce_fusion), channel_id=1, replica_groups=mesh['row'=8,'col'=32] {'col'}, use_global_device_ids=true, to_apply=%region_6.7 | all-reduce | flops 128 | bytes 1024 | tf_op jit(solution)/shard_map/psum | solution.py:27
  403.6 6.1 %multiply_subtract_fusion = f32[1024,832]{0,1:T(8,128)} fusion(f32[1024,128]{1,0:T(8,128)S(1)} %fusion.5, f32[832,128]{1,0:T(8,128)} %all-reduce.8.cloned.1.call-done, f32[1024,832]{0,1:T(8,128)} %param.3, bf16[1024,832]{0,1:T(8,128)(2,1)S(1)} %copy-done.1), kind=kOutput, calls=%fused_computation.1 | convolution fusion | flops 1312030720 | bytes 9469952 | tf_op jit(solution)/shard_map/dot_general | solution.py:29
  409.7 3.9 multiply_convert_fusion
  (7 shorter events, 0.1 us)
Async XLA Ops:
  7.2 1.0 copy-start
  7.2 249.6 %copy-start.1 = (bf16[1024,832]{0,1:T(8,128)(2,1)S(1)}, bf16[1024,832]{0,1:T(8,128)(2,1)}, u32[]{:S(2)}) copy-start(bf16[1024,832]{0,1:T(8,128)(2,1)} %param.4) | copy-start | bytes 5111812
  7.2 159.5 %all-reduce.4.cloned.1.call-start = ((), (), s32[]{:S(2)}) async-start(), calls=%async_computation | async-start | bytes 1048576 | tf_op jit(solution)/shard_map/psum | solution.py:23
  17.9 212.6 %all-reduce.6.cloned.1.call-start = ((), (), s32[]{:S(2)}) async-start(), calls=%async_computation.1 | async-start | bytes 131072 | tf_op jit(solution)/shard_map/psum | solution.py:24
  169.5 157.7 %all-reduce.8.cloned.1.call-start = ((), (), s32[]{:S(2)}) async-start(), calls=%async_computation.2 | async-start | bytes 851968 | tf_op jit(solution)/shard_map/psum | solution.py:26
  403.6 6.1 %copy-start.2 = (f32[832,128]{1,0:T(8,128)S(1)}, f32[832,128]{1,0:T(8,128)}, u32[]{:S(2)}) copy-start(f32[832,128]{1,0:T(8,128)} %all-reduce.8.cloned.1.call-done) | copy-start | bytes 1277956
Sparse Core Ops, SparseCore 0:
  18.0 148.5 all-reduce.3
  169.7 60.8 all-reduce.5
  262.5 64.7 all-reduce.7
where the time goes:
time: 421 us; the launch traced here: 420 us
  waiting for transfers between devices  274 us (65%)
  blocking collectives  75.3 us (18%)
  matrix products  29.7 us (7%)
  other arithmetic  24.8 us (6%)
  between operations  13.8 us (3%)
    psum x1, waiting for transfers between devices, body(): left = lax.psum(jnp.dot(blend, right_factor, precision=high), 'col')  149 us
    psum x1, blocking collectives, body(): colsq = lax.psum(jnp.sum(across * across, axis=0), 'col')  75.3 us
    psum x1, waiting for transfers between devices, body(): across = lax.psum(contract_first(blend, basis), 'row')  64.9 us
    psum x1, waiting for transfers between devices, body(): gram = lax.psum(contract_first(left, left), 'row')  60.8 us
    another operation x3, other arithmetic, orthonormal(): lower = jnp.linalg.cholesky(gram)  12.4 us
    another operation x2, other arithmetic, orthonormal(): lax.linalg.triangular_solve(lower, left, left_side=False, lower=True, tra...  10.5 us
    dot_general x1, matrix products, body(): left = lax.psum(jnp.dot(blend, right_factor, precision=high), 'col')  9.7 us
  transfers between devices with their start and end apart: 3, of which 3 were waited for; matrix products, arithmetic and copies ran while one was open for 0% of the time, Pallas kernels for 0%

commit v1 on v0

v1 whole, which is shorter than its diff:
```python
import jax
import jax.numpy as jnp
from jax import lax
from jax.sharding import PartitionSpec as P

ROWS = 8192
COLS = 26624
RANK = 128
HIGH = lax.Precision.HIGHEST

OTHER_CORE = [(i, i ^ 1) for i in range(8)]
SAME_CORE = [[0, 2, 4, 6], [1, 3, 5, 7]]


def contract_first(first, second):
    return lax.dot_general(first, second, (((0,), (0,)), ((), ())), precision=HIGH)


def exchange(blocks, axis, groups=None):
    return lax.all_to_all(blocks, axis, 0, 0, axis_index_groups=groups)


def spread(block, count, axis, groups=None):
    return exchange(jnp.broadcast_to(block[None], (count,) + block.shape), axis, groups)


def sum_over_col(partial):
    rows = partial.shape[0] // 32
    mine = jnp.sum(exchange(partial.reshape(32, rows, RANK), "col"), axis=0)
    return spread(mine, 32, "col").reshape(partial.shape)


def sum_over_row(partial):
    half = partial.shape[0] // 2
    core = lax.rem(lax.axis_index("row"), 2)
    halves = partial.reshape(2, half, RANK)
    keep = lax.dynamic_index_in_dim(halves, core, 0, keepdims=False)
    give = lax.dynamic_index_in_dim(halves, 1 - core, 0, keepdims=False)
    keep = keep + lax.ppermute(give, "row", OTHER_CORE)
    mine = jnp.sum(exchange(keep.reshape(4, half // 4, RANK), "row", SAME_CORE), axis=0)
    keep = spread(mine, 4, "row", SAME_CORE).reshape(half, RANK)
    theirs = lax.ppermute(keep, "row", OTHER_CORE)
    first = jnp.where(core == 0, keep, theirs)
    second = jnp.where(core == 0, theirs, keep)
    return jnp.concatenate([first, second], axis=0)


def body(momentum, gradient, right_factor):
    blend = momentum + gradient.astype(jnp.float32)
    left = sum_over_col(jnp.dot(blend, right_factor, precision=HIGH))
    both = sum_over_row(jnp.concatenate([contract_first(blend, left), contract_first(left, left)], axis=0))
    weighted, gram = both[:832], both[832:]
    lower = jnp.linalg.cholesky(gram)
    inverse = lax.linalg.triangular_solve(lower, jnp.eye(RANK, dtype=jnp.float32), left_side=True, lower=True)
    basis = jnp.dot(left, inverse.T, precision=HIGH)
    across = jnp.dot(weighted, inverse.T, precision=HIGH)
    colsq = jnp.sum(across * across, axis=0, keepdims=True)
    colsq = jnp.sum(spread(colsq, 32, "col"), axis=0)
    fresh = across / jnp.sqrt(colsq + 1e-06)
    new_momentum = blend - 0.05 * jnp.dot(basis, across.T, precision=HIGH)
    scale_factor = (ROWS * COLS / RANK) ** 0.5
    update = (scale_factor * jnp.dot(basis, fresh.T, precision=HIGH)).astype(jnp.bfloat16)
    return (new_momentum, update)


def solution(mesh):
    in_specs = (P("row", "col"), P("row", "col"), P("col", None))
    out_specs = (P("row", "col"), P("row", "col"))
    return jax.shard_map(body, mesh=mesh, in_specs=in_specs, out_specs=out_specs, check_vma=False)
```

time: 421 us -> 138 us (0.33)
  the two profiles are of different devices: /device:TPU:0 before, /device:TPU:1 now
where the time goes in v1:
time: 138 us; the launch traced here: 137 us
  blocking collectives  43.4 us (31%)
  matrix products  26.3 us (19%)
  other arithmetic  24.8 us (18%)
  starting transfers between devices  20.4 us (15%)
  waiting for transfers between devices  18.6 us (13%)
  local copies, waits for them, and re-layouts  2.82 us (2%)
    all_to_all x3, blocking collectives, exchange(): return lax.all_to_all(blocks, axis, 0, 0, axis_index_groups=groups)  43.4 us
    all_to_all x2, waiting for transfers between devices, exchange(): return lax.all_to_all(blocks, axis, 0, 0, axis_index_groups=groups)  16.2 us
    all_to_all x2, starting transfers between devices, exchange(): return lax.all_to_all(blocks, axis, 0, 0, axis_index_groups=groups)  12.5 us
    another operation x3, other arithmetic, body(): lower = jnp.linalg.cholesky(gram)  12.4 us
    another operation x2, other arithmetic, body(): lax.linalg.triangular_solve(lower, jnp.eye(RANK, dtype=jnp.float32), left...  10.5 us
    dot_general x1, matrix products, body(): left = sum_over_col(jnp.dot(blend, right_factor, precision=HIGH))  7.81 us
    dot_general x1, matrix products, body(): new_momentum = blend - 0.05 * jnp.dot(basis, across.T, precision=HIGH)  5.98 us
    dot_general x2, matrix products, contract_first(): lax.dot_general(first, second, (((0,), (0,)), ((), ())), precision=HIGH)  5.78 us
  transfers between devices with their start and end apart: 4, of which 4 were waited for; matrix products, arithmetic and copies ran while one was open for 4% of the time, Pallas kernels for 0%

profile of v1, /device:TPU:1, one launch (start us, length us, event | category | flops | bytes accessed | tf_op | source)
XLA Modules:
  0.0 137.1 jit_solution(13909907992996318726)
XLA Ops:
  0.7 1.0 copy-done
  1.6 7.8 %fusion.1 = f32[1024,128]{1,0:T(8,128)S(1)} fusion(f32[832,128]{1,0:T(8,128)S(1)} %copy-done, f32[1024,832]{0,1:T(8,128)} %param.3, bf16[1024,832]{0,1:T(8,128)(2,1)} %param.4), kind=kOutput, calls=%fused_computation.4 | convolution fusion | flops 1310326784 | bytes 6062080 | tf_op jit(solution)/shard_map/dot_general | solution.py:50
  9.5 26.0 %all_to_all.25 = f32[32,32,128]{2,1,0:T(8,128)S(1)} all-to-all(f32[32,32,128]{2,1,0:T(8,128)S(1)} %bitcast.33), channel_id=1, replica_groups=mesh['row'=8,'col'=32] {'col'}, dimensions={0} | all-to-all | bytes 1048576 | tf_op jit(solution)/shard_map/all_to_all | solution.py:20
  35.5 0.9 broadcast_in_dim.7
  36.3 7.5 %all-to-all-start.1 = ((f32[32,32,128]{2,1,0:T(8,128)}), f32[32,32,128]{2,1,0:T(8,128)S(1)}, u32[]{:S(2)}, u32[]{:S(2)}) async-start(f32[32,32,128]{2,1,0:T(8,128)} %broadcast_in_dim.7), calls=%async_computation.1 | async-start | bytes 1048576 | tf_op jit(solution)/shard_map/all_to_all | solution.py:20
  43.8 13.6 %all-to-all-done.1 = f32[32,32,128]{2,1,0:T(8,128)S(1)} async-done(((f32[32,32,128]{2,1,0:T(8,128)}), f32[32,32,128]{2,1,0:T(8,128)S(1)}, u32[]{:S(2)}, u32[]{:S(2)}) %all-to-all-start.1) | async-done | bytes 524320 | tf_op jit(solution)/shard_map/all_to_all | solution.py:20
  57.5 4.8 %fusion = f32[832,128]{1,0:T(8,128)S(1)} fusion(f32[1024,128]{1,0:T(8,128)S(1)} %bitcast.31, f32[1024,832]{0,1:T(8,128)} %param.3, bf16[1024,832]{0,1:T(8,128)(2,1)S(1)} %copy-done.1), kind=kOutput, calls=%fused_computation.3 | convolution fusion | flops 1310326784 | bytes 6062080 | tf_op jit(solution)/shard_map/dot_general | solution.py:16
  62.2 1.0 convolution_bitcast_fusion
  63.3 4.6 %collective-permute-start = (f32[480,128]{1,0:T(8,128)S(1)}, f32[480,128]{1,0:T(8,128)}, u32[]{:S(2)}, u32[]{:S(2)}) collective-permute-start(f32[480,128]{1,0:T(8,128)S(1)} %dynamic-slice_bitcast_fusion), channel_id=1, source_target_pairs={{0,32},{32,0},{64,96},{96,64},{128,160},{160,128},{192,224},{224,1... | collective-permute-start | bytes 737288 | tf_op jit(solution)/shard_map/ppermute | solution.py:39
  68.0 1.3 collective-permute-done
  69.2 1.0 bitcast_add_fusion
  70.2 9.6 %all_to_all.26 = f32[4,120,128]{2,1,0:T(8,128)S(1)} all-to-all(f32[4,120,128]{2,1,0:T(8,128)S(1)} %bitcast.36), channel_id=1, replica_groups={{0,64,128,192},{32,96,160,224},{1,65,129,193},{33,97,161,225},{2,66,130..., dimensions={0} | all-to-all | bytes 491520 | tf_op jit(solution)/shard_map/all_to_all | solution.py:20
  79.9 7.8 %all_to_all.27 = f32[4,120,128]{2,1,0:T(8,128)S(1)} all-to-all(f32[4,120,128]{2,1,0:T(8,128)S(1)} %broadcast_in_dim.8), channel_id=1, replica_groups={{0,64,128,192},{32,96,160,224},{1,65,129,193},{33,97,161,225},{2,66,130..., dimensions={0} | all-to-all | bytes 491520 | tf_op jit(solution)/shard_map/all_to_all | solution.py:20
  87.8 3.2 %collective-permute-start.1 = (f32[480,128]{0,1:T(8,128)S(1)}, f32[480,128]{0,1:T(8,128)S(1)}, u32[]{:S(2)}, u32[]{:S(2)}) collective-permute-start(f32[480,128]{0,1:T(8,128)S(1)} %copy.14), channel_id=1, source_target_pairs={{0,32},{32,0},{64,96},{96,64},{128,160},{160,128},{192,224},{224,1... | collective-permute-start | bytes 737288 | tf_op jit(solution)/shard_map/ppermute | solution.py:42
  91.1 1.2 collective-permute-done.1
  92.2 0.7 broadcast_select_fusion
  93.3 11.7 %cholesky.17 = f32[128,128]{1,0:T(8,128)S(1)} custom-call(f32[128,128]{1,0:T(8,128)S(1)} %fusion.9), custom_call_target="Cholesky" | custom-call | tf_op jit(solution)/shard_map/jit(cholesky)/cholesky | solution.py:53
  105.6 0.7 fusion.6
  106.3 9.8 %custom-call.6 = f32[1,128,128]{1,2,0:T(8,128)S(1)} custom-call(f32[1,128,128]{2,1,0:T(8,128)S(1)} %fusion.6), custom_call_target="InvertDiagBlocksLowerTriangular" | custom-call | tf_op jit(solution)/shard_map/triangular_solve | solution.py:54
  117.0 1.9 %multiply_reduce_fusion = (f32[128]{0:T(128)S(1)}, f32[832,128]{1,0:T(8,128)S(1)}) fusion(f32[128,128]{1,0:T(8,128)S(1)} %fusion.7, f32[480,128]{0,1:T(8,128)S(1)} %get-tuple-element.3, f32[480,128]{0,1:T(8,128)} %get-tuple-element.2), kind=kOutput, calls=%fused_computation.11 | convolution fusion | flops 163897216 | bytes 983552 | tf_op jit(solution)/shard_map/dot_general | solution.py:56
  119.5 5.0 %all-to-all-start.4 = ((f32[32,1,128]{2,1,0:T(1,128)}), f32[32,1,128]{2,1,0:T(1,128)S(1)}, u32[]{:S(2)}, u32[]{:S(2)}) async-start(f32[32,1,128]{2,1,0:T(1,128)} %broadcast_in_dim.10), calls=%async_computation.4 | async-start | bytes 32768 | tf_op jit(solution)/shard_map/all_to_all | solution.py:20
  124.5 6.0 %multiply_subtract_fusion = f32[1024,832]{0,1:T(8,128)} fusion(f32[1024,128]{1,0:T(8,128)S(1)} %fusion.11, f32[832,128]{1,0:T(8,128)S(1)} %get-tuple-element.5, f32[1024,832]{0,1:T(8,128)} %param.3, bf16[1024,832]{0,1:T(8,128)(2,1)S(1)} %copy-done.1), kind=kOutput, calls=%fused_computation.1 | convolution fusion | flops 1312030720 | bytes 9469952 | tf_op jit(solution)/shard_map/dot_general | solution.py:60
  130.5 2.6 %all-to-all-done.4 = f32[32,1,128]{2,1,0:T(1,128)S(1)} async-done(((f32[32,1,128]{2,1,0:T(1,128)}), f32[32,1,128]{2,1,0:T(1,128)S(1)}, u32[]{:S(2)}, u32[]{:S(2)}) %all-to-all-start.4) | async-done | bytes 16416 | tf_op jit(solution)/shard_map/all_to_all | solution.py:20
  133.1 4.0 %multiply_convert_fusion = bf16[1024,832]{0,1:T(8,128)(2,1)} fusion(f32[1024,128]{1,0:T(8,128)S(1)} %fusion.11, f32[832,128]{1,0:T(8,128)S(1)} %get-tuple-element.5, f32[128]{0:T(128)S(1)} %add_sqrt_fusion), kind=kOutput, calls=%fused_computation | convolution fusion | flops 1310433280 | bytes 2654720 | tf_op jit(solution)/shard_map/dot_general | solution.py:62
  (19 shorter events, 2.7 us)
Async XLA Ops:
  0.6 1.0 copy-start
  0.6 56.8 %copy-start.1 = (bf16[1024,832]{0,1:T(8,128)(2,1)S(1)}, bf16[1024,832]{0,1:T(8,128)(2,1)}, u32[]{:S(2)}) copy-start(bf16[1024,832]{0,1:T(8,128)(2,1)} %param.4) | copy-start | bytes 5111812
  36.3 21.1 %all-to-all-start.1 = ((f32[32,32,128]{2,1,0:T(8,128)}), f32[32,32,128]{2,1,0:T(8,128)S(1)}, u32[]{:S(2)}, u32[]{:S(2)}) async-start(f32[32,32,128]{2,1,0:T(8,128)} %broadcast_in_dim.7), calls=%async_computation.1 | async-start | bytes 1048576 | tf_op jit(solution)/shard_map/all_to_all | solution.py:20
  63.3 5.9 %collective-permute-start = (f32[480,128]{1,0:T(8,128)S(1)}, f32[480,128]{1,0:T(8,128)}, u32[]{:S(2)}, u32[]{:S(2)}) collective-permute-start(f32[480,128]{1,0:T(8,128)S(1)} %dynamic-slice_bitcast_fusion), channel_id=1, source_target_pairs={{0,32},{32,0},{64,96},{96,64},{128,160},{160,128},{192,224},{224,1... | collective-permute-start | bytes 737288 | tf_op jit(solution)/shard_map/ppermute | solution.py:39
  87.8 4.4 %collective-permute-start.1 = (f32[480,128]{0,1:T(8,128)S(1)}, f32[480,128]{0,1:T(8,128)S(1)}, u32[]{:S(2)}, u32[]{:S(2)}) collective-permute-start(f32[480,128]{0,1:T(8,128)S(1)} %copy.14), channel_id=1, source_target_pairs={{0,32},{32,0},{64,96},{96,64},{128,160},{160,128},{192,224},{224,1... | collective-permute-start | bytes 737288 | tf_op jit(solution)/shard_map/ppermute | solution.py:42
  119.5 13.6 %all-to-all-start.4 = ((f32[32,1,128]{2,1,0:T(1,128)}), f32[32,1,128]{2,1,0:T(1,128)S(1)}, u32[]{:S(2)}, u32[]{:S(2)}) async-start(f32[32,1,128]{2,1,0:T(1,128)} %broadcast_in_dim.10), calls=%async_computation.4 | async-start | bytes 32768 | tf_op jit(solution)/shard_map/all_to_all | solution.py:20

commit v2 on v0

v2 whole, which is shorter than its diff:
```python
import jax
import jax.numpy as jnp
from jax import lax
from jax.experimental import pallas as pl
from jax.experimental.pallas import tpu as pltpu
from jax.sharding import PartitionSpec as P

ROWS = 8192
COLS = 26624
RANK = 128
HIGH = lax.Precision.HIGHEST
F32 = jnp.float32
BF16 = jnp.bfloat16

C = 832
R = 1024
STEPS = 4
BLOCK = 16

CORE, NEAR, FAR = 1, 2, 6


def dot(first, second, dims=((1,), (0,)), precision=None):
    return lax.dot_general(first, second, (dims, ((), ())), precision=precision, preferred_element_type=F32)


def split(x):
    high = x.astype(BF16)
    return high, (x - high.astype(F32)).astype(BF16)


def params(mib):
    return pltpu.CompilerParams(vmem_limit_bytes=mib << 20)


def left_kernel(m_ref, g_ref, r_ref, left_ref, blend_ref, both_ref):
    @pl.when(pl.program_id(0) == 0)
    def _():
        high, low = split(r_ref[...].T)
        both_ref[:RANK] = high
        both_ref[RANK:] = low

    blend = m_ref[...] + g_ref[...].astype(F32)
    blend_ref[...] = blend
    high, low = split(blend)
    wide = dot(both_ref[...], high)
    left_ref[...] = (wide[:RANK] + wide[RANK:] + dot(both_ref[:RANK], low)).T


def left_of(m, g, r):
    width = R // STEPS
    return pl.pallas_call(
        left_kernel,
        grid=(STEPS,),
        in_specs=[
            pl.BlockSpec((C, width), lambda i: (0, i)),
            pl.BlockSpec((C, width), lambda i: (0, i)),
            pl.BlockSpec((C, RANK), lambda i: (0, 0)),
        ],
        out_specs=[
            pl.BlockSpec((width, RANK), lambda i: (i, 0)),
            pl.BlockSpec((C, width), lambda i: (0, i)),
        ],
        out_shape=[jax.ShapeDtypeStruct((R, RANK), F32), jax.ShapeDtypeStruct((C, R), F32)],
        scratch_shapes=[pltpu.VMEM((2 * RANK, C), BF16)],
        compiler_params=params(24),
        cost_estimate=pl.CostEstimate(flops=6 * R * C * RANK, bytes_accessed=R * C * 10, transcendentals=0),
        name="left_part",
    )(m, g, r)


def gram_kernel(left_ref, out_ref):
    left = left_ref[...]
    out_ref[...] = dot(left, left, ((0,), (0,)), HIGH)


def gram_of(left):
    return pl.pallas_call(
        gram_kernel,
        out_shape=jax.ShapeDtypeStruct((RANK, RANK), F32),
        compiler_params=params(16),
        cost_estimate=pl.CostEstimate(flops=12 * R * RANK * RANK, bytes_accessed=R * RANK * 4, transcendentals=0),
        name="gram_part",
    )(left)


def weighted_kernel(blend_ref, left_ref, out_ref, both_ref):
    @pl.when(pl.program_id(0) == 0)
    def _():
        high, low = split(left_ref[...])
        both_ref[:, :RANK] = high
        both_ref[:, RANK:] = low

    high, low = split(blend_ref[...])
    wide = dot(high, both_ref[...])
    out_ref[...] = wide[:, :RANK] + wide[:, RANK:] + dot(low, both_ref[:, :RANK])


def weighted_of(blend, left):
    height = C // STEPS
    return pl.pallas_call(
        weighted_kernel,
        grid=(STEPS,),
        in_specs=[
            pl.BlockSpec((height, R), lambda i: (i, 0)),
            pl.BlockSpec((R, RANK), lambda i: (0, 0)),
        ],
        out_specs=pl.BlockSpec((height, RANK), lambda i: (i, 0)),
        out_shape=jax.ShapeDtypeStruct((C, RANK), F32),
        scratch_shapes=[pltpu.VMEM((R, 2 * RANK), BF16)],
        compiler_params=params(16),
        cost_estimate=pl.CostEstimate(flops=6 * R * C * RANK, bytes_accessed=R * C * 4, transcendentals=0),
        name="weighted_part",
    )(blend, left)


def inverse_kernel(gram_ref, out_ref, work_ref):
    n, b = RANK, BLOCK
    row = lax.broadcasted_iota(jnp.int32, (n, n), 0)
    column = lax.broadcasted_iota(jnp.int32, (n, n), 1)
    work_ref[:, :n] = gram_ref[...]
    work_ref[:, n:] = jnp.where(row == column, 1.0, 0.0)
    place = lax.broadcasted_iota(jnp.int32, (b, n), 0)
    for o in range(0, n, b):
        upper, inverse = work_ref[o : o + b, :n], work_ref[o : o + b, n:]
        columns = [jnp.broadcast_to(upper[:, o + j : o + j + 1], (b, n)) for j in range(b)]
        pivots = jnp.zeros((b, n), F32)
        for i in range(b):
            pivot = 1.0 / jnp.broadcast_to(columns[i][i : i + 1], (b, n))
            pivots = jnp.where(place == i, pivot, pivots)
            if i + 1 < b:
                factor = jnp.where(place > i, columns[i] * pivot, 0.0)
                for j in range(i + 1, b):
                    columns[j] = columns[j] - factor * columns[j][i : i + 1]
                upper = upper - factor * upper[i : i + 1]
                inverse = inverse - factor * inverse[i : i + 1]
        root = jnp.sqrt(pivots)
        upper, inverse = upper * root, inverse * root
        out_ref[o : o + b] = inverse
        if o + b < n:
            done = jnp.concatenate([upper, inverse], axis=1)
            work_ref[o + b :] -= dot(upper[:, o + b :], done, ((0,), (0,)), HIGH)


def inverse_of(gram):
    return pl.pallas_call(
        inverse_kernel,
        out_shape=jax.ShapeDtypeStruct((RANK, RANK), F32),
        scratch_shapes=[pltpu.VMEM((RANK, 2 * RANK), F32)],
        compiler_params=params(16),
        cost_estimate=pl.CostEstimate(flops=6 << 30, bytes_accessed=1 << 17, transcendentals=0),
        name="inverse_factor",
    )(gram)


def across_kernel(weighted_ref, inverse_ref, across_ref, colsq_ref):
    across = dot(weighted_ref[...], inverse_ref[...], ((1,), (1,)), HIGH)
    across_ref[...] = across
    colsq_ref[...] = jnp.broadcast_to(jnp.sum(across * across, axis=0, keepdims=True), colsq_ref.shape)


def across_of(weighted, inverse):
    return pl.pallas_call(
        across_kernel,
        out_shape=[jax.ShapeDtypeStruct((C, RANK), F32), jax.ShapeDtypeStruct((32, RANK), F32)],
        compiler_params=params(16),
        cost_estimate=pl.CostEstimate(flops=12 * C * RANK * RANK, bytes_accessed=C * RANK * 8, transcendentals=0),
        name="across_part",
    )(weighted, inverse)


def momentum_kernel(blend_ref, left_ref, inverse_ref, across_ref, new_ref, basis_ref):
    @pl.when(pl.program_id(0) == 0)
    def _():
        high, low = split(dot(inverse_ref[...], left_ref[...], ((1,), (1,)), HIGH))
        basis_ref[:RANK] = high
        basis_ref[RANK:] = low

    wide = jnp.concatenate(split(across_ref[...] * 0.05), axis=1)
    high = basis_ref[:RANK]
    new_ref[...] = blend_ref[...] - dot(wide, jnp.concatenate([high, high], axis=0))


def momentum_of(blend, left, inverse, across):
    height = C // STEPS
    return pl.pallas_call(
        momentum_kernel,
        grid=(STEPS,),
        in_specs=[
            pl.BlockSpec((height, R), lambda i: (i, 0)),
            pl.BlockSpec((R, RANK), lambda i: (0, 0)),
            pl.BlockSpec((RANK, RANK), lambda i: (0, 0)),
            pl.BlockSpec((height, RANK), lambda i: (i, 0)),
        ],
        out_specs=[
            pl.BlockSpec((height, R), lambda i: (i, 0)),
            pl.BlockSpec((2 * RANK, R), lambda i: (0, 0)),
        ],
        out_shape=[jax.ShapeDtypeStruct((C, R), F32), jax.ShapeDtypeStruct((2 * RANK, R), BF16)],
        compiler_params=params(24),
        cost_estimate=pl.CostEstimate(flops=4 * R * C * RANK, bytes_accessed=R * C * 8, transcendentals=0),
        name="new_momentum",
    )(blend, left, inverse, across)


def update_kernel(across_ref, colsq_ref, basis_ref, update_ref):
    colsq = jnp.sum(colsq_ref[...], axis=0, keepdims=True)
    scale_factor = (ROWS * COLS / RANK) ** 0.5
    high, low = split(across_ref[...] * (scale_factor / jnp.sqrt(colsq + 1e-06)))
    basis_high, basis_low = basis_ref[:RANK], basis_ref[RANK:]
    wide = jnp.concatenate([high, low], axis=1)
    product = dot(wide, jnp.concatenate([basis_high, basis_high], axis=0)) + dot(high, basis_low)
    update_ref[...] = product.astype(BF16)


def update_of(across, colsq, basis):
    height = C // STEPS
    return pl.pallas_call(
        update_kernel,
        grid=(STEPS,),
        in_specs=[
            pl.BlockSpec((height, RANK), lambda i: (i, 0)),
            pl.BlockSpec((32, RANK), lambda i: (0, 0)),
            pl.BlockSpec((2 * RANK, R), lambda i: (0, 0)),
        ],
        out_specs=pl.BlockSpec((height, R), lambda i: (i, 0)),
        out_shape=jax.ShapeDtypeStruct((C, R), BF16),
        compiler_params=params(16),
        cost_estimate=pl.CostEstimate(flops=6 * R * C * RANK, bytes_accessed=R * C * 2, transcendentals=0),
        name="update",
    )(across, colsq, basis)


def exchange(blocks, axis):
    return lax.all_to_all(blocks, axis, 0, 0)


def sum_over_col(partial):
    rows = partial.shape[0] // 32
    mine = jnp.sum(exchange(partial.reshape(32, rows, RANK), "col"), axis=0)
    return exchange(jnp.broadcast_to(mine[None], (32, rows, RANK)), "col").reshape(partial.shape)


def swap(x, flip):
    return lax.ppermute(x, "row", [(i, i ^ flip) for i in range(8)])


def sum_over_row(weighted, gram):
    core = lax.rem(lax.axis_index("row"), 2)
    gram = gram + swap(gram, CORE)
    halves = weighted.reshape(2, C // 2, RANK)
    keep = lax.dynamic_index_in_dim(halves, core, 0, keepdims=False)
    give = lax.dynamic_index_in_dim(halves, 1 - core, 0, keepdims=False)
    keep = keep + swap(give, CORE)
    gram = gram + swap(gram, NEAR)
    gram = gram + swap(gram, FAR)
    first, second = keep[: C // 4], keep[C // 4 :]
    first = first + swap(first, NEAR)
    second = second + swap(second, FAR)
    first = first + swap(first, FAR)
    second = second + swap(second, NEAR)
    keep = jnp.concatenate([first, second], axis=0)
    theirs = swap(keep, CORE)
    upper = jnp.where(core == 0, keep, theirs)
    lower = jnp.where(core == 0, theirs, keep)
    return jnp.concatenate([upper, lower], axis=0), gram


def body(momentum, gradient, right_factor):
    partial, blend = left_of(momentum.T, gradient.T, right_factor)
    left = sum_over_col(partial)
    weighted, gram = sum_over_row(weighted_of(blend, left), gram_of(left))
    inverse = inverse_of(gram)
    across, colsq = across_of(weighted, inverse)
    colsq = exchange(colsq.reshape(32, 1, RANK), "col").reshape(32, RANK)
    new_momentum, basis = momentum_of(blend, left, inverse, across)
    update = update_of(across, colsq, basis)
    return (new_momentum.T, update.T)


def solution(mesh):
    in_specs = (P("row", "col"), P("row", "col"), P("col", None))
    out_specs = (P("row", "col"), P("row", "col"))
    return jax.shard_map(body, mesh=mesh, in_specs=in_specs, out_specs=out_specs, check_vma=False)
```

time: 421 us -> 115 us (0.27)
  the two profiles are of different devices: /device:TPU:0 before, /device:TPU:1 now
where the time goes in v2:
time: 115 us; the launch traced here: 114 us
  starting transfers between devices  27 us (23%)
  blocking collectives  26.1 us (23%)
  waiting for transfers between devices  22.8 us (20%)
  Pallas kernels  20 us (17%)
  local copies, waits for them, and re-layouts  11.3 us (10%)
  other arithmetic  6.29 us (5%)
    all_to_all x1, blocking collectives, exchange(): return lax.all_to_all(blocks, axis, 0, 0)  26.1 us
    all_to_all x2, waiting for transfers between devices, exchange(): return lax.all_to_all(blocks, axis, 0, 0)  16.1 us
    ppermute x9, starting transfers between devices, swap(): return lax.ppermute(x, 'row', [(i, i ^ flip) for i in range(8)])  14.4 us
    all_to_all x2, starting transfers between devices, exchange(): return lax.all_to_all(blocks, axis, 0, 0)  12.6 us
    unnamed x18, local copies, waits for them, and re-layouts  9.77 us
    ppermute x9, waiting for transfers between devices, swap(): return lax.ppermute(x, 'row', [(i, i ^ flip) for i in range(8)])  6.68 us
    pallas_call x1, Pallas kernels, inverse_of(): pl.pallas_call(inverse_kernel, out_shape=jax.ShapeDtypeStruct((RANK, RANK...  4.73 us
    pallas_call x1, Pallas kernels, momentum_of(): pl.pallas_call(momentum_kernel, grid=(STEPS,), in_specs=[pl.BlockSpec((he...  4.28 us
  transfers between devices with their start and end apart: 11, of which 6 were waited for; matrix products, arithmetic and copies ran while one was open for 3% of the time, Pallas kernels for 9%

profile of v2, /device:TPU:1, one launch (start us, length us, event | category | flops | bytes accessed | tf_op | source)
XLA Modules:
  0.0 114.3 jit_solution(9977203728350427796)
XLA Ops:
  0.6 2.0 %copy-done = f32[1024,832]{0,1:T(8,128)S(1)} copy-done((f32[1024,832]{0,1:T(8,128)S(1)}, f32[1024,832]{0,1:T(8,128)}, u32[]{:S(2)}) %copy-start) | copy-done | bytes 3407896
  2.6 1.5 %copy-done.5 = bf16[1024,832]{0,1:T(8,128)(2,1)S(1)} copy-done((bf16[1024,832]{0,1:T(8,128)(2,1)S(1)}, bf16[1024,832]{0,1:T(8,128)(2,1)}, u32[]{:S(2)}) %copy-start.5) | copy-done | bytes 1703960
  5.1 2.8 %left_part.1 = (f32[1024,128]{1,0:T(8,128)S(1)}, f32[832,1024]{1,0:T(8,128)S(1)}) custom-call(f32[832,1024]{1,0:T(8,128)S(1)} %bitcast.15, bf16[832,1024]{1,0:T(8,128)(2,1)S(1)} %bitcast.18, f32[832,128]{1,0:T(8,128)S(1)} %copy-done.8), custom_call_target="tpu_custom_call" | custom-call | flops 654311424 | bytes 8519680 | tf_op jit(solution)/shard_map/left_part/pallas_call | solution.py:52
  7.9 26.1 %all_to_all.15 = f32[32,32,128]{2,1,0:T(8,128)} all-to-all(f32[32,32,128]{2,1,0:T(8,128)S(1)} %bitcast.19), channel_id=1, replica_groups=mesh['row'=8,'col'=32] {'col'}, dimensions={0} | all-to-all | bytes 1048576 | tf_op jit(solution)/shard_map/all_to_all | solution.py:235
  33.9 1.1 reduce_sum.9
  35.9 7.6 %all-to-all-start.1 = ((f32[32,32,128]{2,1,0:T(8,128)}), f32[32,32,128]{2,1,0:T(8,128)}, u32[]{:S(2)}, u32[]{:S(2)}) async-start(f32[32,32,128]{2,1,0:T(8,128)} %broadcast_in_dim.2), calls=%async_computation.1 | async-start | bytes 1048576 | tf_op jit(solution)/shard_map/all_to_all | solution.py:235
  43.5 13.6 %all-to-all-done.1 = f32[32,32,128]{2,1,0:T(8,128)} async-done(((f32[32,32,128]{2,1,0:T(8,128)}), f32[32,32,128]{2,1,0:T(8,128)}, u32[]{:S(2)}, u32[]{:S(2)}) %all-to-all-start.1) | async-done | bytes 524320 | tf_op jit(solution)/shard_map/all_to_all | solution.py:235
  57.1 2.7 %weighted_part.1 = f32[832,128]{1,0:T(8,128)S(1)} custom-call(f32[832,1024]{1,0:T(8,128)S(1)} %get-tuple-element.8.blend_ref, f32[1024,128]{1,0:T(8,128)} %bitcast.3.left_ref), custom_call_target="tpu_custom_call" | custom-call | flops 654311424 | bytes 3407872 | tf_op jit(solution)/shard_map/weighted_part/pallas_call | solution.py:101
  61.3 4.5 %collective-permute-start.3 = (f32[416,128]{1,0:T(8,128)}, f32[416,128]{1,0:T(8,128)}, u32[]{:S(2)}, u32[]{:S(2)}) collective-permute-start(f32[416,128]{1,0:T(8,128)} %dynamic-slice_bitcast_fusion), channel_id=1, source_target_pairs={{0,32},{32,0},{64,96},{96,64},{128,160},{160,128},{192,224},{224,1... | collective-permute-start | bytes 638984 | tf_op jit(solution)/shard_map/ppermute | solution.py:245
  65.8 1.4 %collective-permute-done.3 = f32[416,128]{1,0:T(8,128)} collective-permute-done((f32[416,128]{1,0:T(8,128)}, f32[416,128]{1,0:T(8,128)}, u32[]{:S(2)}, u32[]{:S(2)}) %collective-permute-start.3) | collective-permute-done | bytes 213024 | tf_op jit(solution)/shard_map/ppermute | solution.py:245
  67.3 1.1 bitcast_add_fusion
  68.3 1.4 %collective-permute-start.4 = (f32[208,128]{1,0:T(8,128)S(1)}, f32[208,128]{1,0:T(8,128)S(1)}, u32[]{:S(2)}, u32[]{:S(2)}) collective-permute-start(f32[208,128]{1,0:T(8,128)S(1)} %get-tuple-element.18), channel_id=1, source_target_pairs={{0,64},{32,96},{64,0},{96,32},{128,192},{160,224},{192,128},{224,1... | collective-permute-start | bytes 319496 | tf_op jit(solution)/shard_map/ppermute | solution.py:245
  69.7 1.9 %collective-permute-start.6 = (f32[208,128]{1,0:T(8,128)S(1)}, f32[208,128]{1,0:T(8,128)S(1)}, u32[]{:S(2)}, u32[]{:S(2)}) collective-permute-start(f32[208,128]{1,0:T(8,128)S(1)} %get-tuple-element.19), channel_id=1, source_target_pairs={{0,192},{32,224},{64,128},{96,160},{128,64},{160,96},{192,0},{224,... | collective-permute-start | bytes 319496 | tf_op jit(solution)/shard_map/ppermute | solution.py:245
  71.6 1.7 %gram_part.1 = f32[128,128]{1,0:T(8,128)S(1)} custom-call(f32[1024,128]{1,0:T(8,128)} %bitcast.3.left_ref), custom_call_target="tpu_custom_call" | custom-call | flops 201326592 | bytes 524288 | tf_op jit(solution)/shard_map/gram_part/pallas_call | solution.py:78
  79.1 1.1 collective-permute-start.2
  80.2 3.5 %collective-permute-done.2 = f32[128,128]{1,0:T(8,128)} collective-permute-done((f32[128,128]{1,0:T(8,128)}, f32[128,128]{1,0:T(8,128)}, u32[]{:S(2)}, u32[]{:S(2)}) %collective-permute-start.2) | collective-permute-done | bytes 65568 | tf_op jit(solution)/shard_map/ppermute | solution.py:245
  86.5 2.7 %collective-permute-start.8 = (f32[416,128]{1,0:T(8,128)S(1)}, f32[416,128]{1,0:T(8,128)S(1)}, u32[]{:S(2)}, u32[]{:S(2)}) collective-permute-start(f32[416,128]{1,0:T(8,128)S(1)} %pad_maximum_fusion.1), channel_id=1, source_target_pairs={{0,32},{32,0},{64,96},{96,64},{128,160},{160,128},{192,224},{224,1... | collective-permute-start | bytes 638984 | tf_op jit(solution)/shard_map/ppermute | solution.py:245
  89.3 4.7 %inverse_factor.1.inverse_ref = f32[128,128]{1,0:T(8,128)S(1)} custom-call(f32[128,128]{1,0:T(8,128)S(1)} %add.34.gram_ref), custom_call_target="tpu_custom_call" | custom-call | flops 6442450944 | bytes 131072 | tf_op jit(solution)/shard_map/inverse_factor/pallas_call | solution.py:146
  94.1 1.1 across_part.1
  96.0 5.0 %all-to-all-start.2 = ((f32[32,1,128]{2,1,0:T(1,128)}), f32[32,1,128]{2,1,0:T(1,128)S(1)}, u32[]{:S(2)}, u32[]{:S(2)}) async-start(f32[32,1,128]{2,1,0:T(1,128)} %bitcast.9), calls=%async_computation.2 | async-start | bytes 32768 | tf_op jit(solution)/shard_map/all_to_all | solution.py:235
  102.0 4.3 %new_momentum.1 = (f32[832,1024]{1,0:T(8,128)}, bf16[256,1024]{1,0:T(8,128)(2,1)S(1)}) custom-call(f32[832,1024]{1,0:T(8,128)S(1)} %get-tuple-element.8.blend_ref, f32[1024,128]{1,0:T(8,128)} %bitcast.3.left_ref, f32[128,128]{1,0:T(8,128)S(1)} %inverse_factor.1.inverse_ref, f32[832,128]{1,0:T(8,128)S(1)} %copy-done.2), custom_call_target="tpu_custom_call" | custom-call | flops 436207616 | bytes 6815744 | tf_op jit(solution)/shard_map/new_momentum/pallas_call | solution.py:186
  107.1 2.5 %all-to-all-done.2 = f32[32,1,128]{2,1,0:T(1,128)S(1)} async-done(((f32[32,1,128]{2,1,0:T(1,128)}), f32[32,1,128]{2,1,0:T(1,128)S(1)}, u32[]{:S(2)}, u32[]{:S(2)}) %all-to-all-start.2) | async-done | bytes 16416 | tf_op jit(solution)/shard_map/all_to_all | solution.py:235
  110.6 1.0 copy-done.7
  111.7 2.7 %update.1 = bf16[832,1024]{1,0:T(8,128)(2,1)} custom-call(f32[832,128]{1,0:T(8,128)S(1)} %copy-done.3, f32[32,128]{1,0:T(8,128)S(1)} %bitcast.20, bf16[256,1024]{1,0:T(8,128)(2,1)S(1)} %copy-done.7), custom_call_target="tpu_custom_call" | custom-call | flops 654311424 | bytes 1703936 | tf_op jit(solution)/shard_map/update/pallas_call | solution.py:218
  (38 shorter events, 15.5 us)
Async XLA Ops:
  0.6 2.0 %copy-start = (f32[1024,832]{0,1:T(8,128)S(1)}, f32[1024,832]{0,1:T(8,128)}, u32[]{:S(2)}) copy-start(f32[1024,832]{0,1:T(8,128)} %param.3) | copy-start | bytes 10223620
  2.6 1.5 %copy-start.5 = (bf16[1024,832]{0,1:T(8,128)(2,1)S(1)}, bf16[1024,832]{0,1:T(8,128)(2,1)}, u32[]{:S(2)}) copy-start(bf16[1024,832]{0,1:T(8,128)(2,1)} %param.4) | copy-start | bytes 5111812
  4.0 1.0 copy-start.8
  35.9 21.2 %all-to-all-start.1 = ((f32[32,32,128]{2,1,0:T(8,128)}), f32[32,32,128]{2,1,0:T(8,128)}, u32[]{:S(2)}, u32[]{:S(2)}) async-start(f32[32,32,128]{2,1,0:T(8,128)} %broadcast_in_dim.2), calls=%async_computation.1 | async-start | bytes 1048576 | tf_op jit(solution)/shard_map/all_to_all | solution.py:235
  59.8 0.8 copy-start.4
  61.3 6.0 %collective-permute-start.3 = (f32[416,128]{1,0:T(8,128)}, f32[416,128]{1,0:T(8,128)}, u32[]{:S(2)}, u32[]{:S(2)}) collective-permute-start(f32[416,128]{1,0:T(8,128)} %dynamic-slice_bitcast_fusion), channel_id=1, source_target_pairs={{0,32},{32,0},{64,96},{96,64},{128,160},{160,128},{192,224},{224,1... | collective-permute-start | bytes 638984 | tf_op jit(solution)/shard_map/ppermute | solution.py:245
  68.3 7.4 %collective-permute-start.4 = (f32[208,128]{1,0:T(8,128)S(1)}, f32[208,128]{1,0:T(8,128)S(1)}, u32[]{:S(2)}, u32[]{:S(2)}) collective-permute-start(f32[208,128]{1,0:T(8,128)S(1)} %get-tuple-element.18), channel_id=1, source_target_pairs={{0,64},{32,96},{64,0},{96,32},{128,192},{160,224},{192,128},{224,1... | collective-permute-start | bytes 319496 | tf_op jit(solution)/shard_map/ppermute | solution.py:245
  69.7 6.0 %collective-permute-start.6 = (f32[208,128]{1,0:T(8,128)S(1)}, f32[208,128]{1,0:T(8,128)S(1)}, u32[]{:S(2)}, u32[]{:S(2)}) collective-permute-start(f32[208,128]{1,0:T(8,128)S(1)} %get-tuple-element.19), channel_id=1, source_target_pairs={{0,192},{32,224},{64,128},{96,160},{128,64},{160,96},{192,0},{224,... | collective-permute-start | bytes 319496 | tf_op jit(solution)/shard_map/ppermute | solution.py:245
  73.3 1.9 %collective-permute-start = (f32[128,128]{1,0:T(8,128)S(1)}, f32[128,128]{1,0:T(8,128)S(1)}, u32[]{:S(2)}, u32[]{:S(2)}) collective-permute-start(f32[128,128]{1,0:T(8,128)S(1)} %gram_part.1), channel_id=1, source_target_pairs={{0,32},{32,0},{64,96},{96,64},{128,160},{160,128},{192,224},{224,1... | collective-permute-start | bytes 196616 | tf_op jit(solution)/shard_map/ppermute | solution.py:245
  75.2 3.2 %collective-permute-start.1 = (f32[128,128]{1,0:T(8,128)S(1)}, f32[128,128]{1,0:T(8,128)S(1)}, u32[]{:S(2)}, u32[]{:S(2)}) collective-permute-start(f32[128,128]{1,0:T(8,128)S(1)} %add.32), channel_id=1, source_target_pairs={{0,64},{32,96},{64,0},{96,32},{128,192},{160,224},{192,128},{224,1... | collective-permute-start | bytes 196616 | tf_op jit(solution)/shard_map/ppermute | solution.py:245
  76.4 8.2 %collective-permute-start.5 = (f32[208,128]{1,0:T(8,128)}, f32[208,128]{1,0:T(8,128)}, u32[]{:S(2)}, u32[]{:S(2)}) collective-permute-start(f32[208,128]{1,0:T(8,128)} %get-tuple-element.16), channel_id=1, source_target_pairs={{0,192},{32,224},{64,128},{96,160},{128,64},{160,96},{192,0},{224,... | collective-permute-start | bytes 319496 | tf_op jit(solution)/shard_map/ppermute | solution.py:245
  77.4 8.2 %collective-permute-start.7 = (f32[208,128]{1,0:T(8,128)S(1)}, f32[208,128]{1,0:T(8,128)}, u32[]{:S(2)}, u32[]{:S(2)}) collective-permute-start(f32[208,128]{1,0:T(8,128)S(1)} %get-tuple-element.17), channel_id=1, source_target_pairs={{0,64},{32,96},{64,0},{96,32},{128,192},{160,224},{192,128},{224,1... | collective-permute-start | bytes 319496 | tf_op jit(solution)/shard_map/ppermute | solution.py:245
  79.1 4.6 %collective-permute-start.2 = (f32[128,128]{1,0:T(8,128)}, f32[128,128]{1,0:T(8,128)}, u32[]{:S(2)}, u32[]{:S(2)}) collective-permute-start(f32[128,128]{1,0:T(8,128)} %add.33), channel_id=1, source_target_pairs={{0,192},{32,224},{64,128},{96,160},{128,64},{160,96},{192,0},{224,... | collective-permute-start | bytes 196616 | tf_op jit(solution)/shard_map/ppermute | solution.py:245
  86.5 7.5 %collective-permute-start.8 = (f32[416,128]{1,0:T(8,128)S(1)}, f32[416,128]{1,0:T(8,128)S(1)}, u32[]{:S(2)}, u32[]{:S(2)}) collective-permute-start(f32[416,128]{1,0:T(8,128)S(1)} %pad_maximum_fusion.1), channel_id=1, source_target_pairs={{0,32},{32,0},{64,96},{96,64},{128,160},{160,128},{192,224},{224,1... | collective-permute-start | bytes 638984 | tf_op jit(solution)/shard_map/ppermute | solution.py:245
  95.2 0.8 copy-start.1
  96.0 13.6 %all-to-all-start.2 = ((f32[32,1,128]{2,1,0:T(1,128)}), f32[32,1,128]{2,1,0:T(1,128)S(1)}, u32[]{:S(2)}, u32[]{:S(2)}) async-start(f32[32,1,128]{2,1,0:T(1,128)} %bitcast.9), calls=%async_computation.2 | async-start | bytes 32768 | tf_op jit(solution)/shard_map/all_to_all | solution.py:235
  101.0 1.0 copy-start.2
  106.3 0.8 copy-start.6
  109.6 1.0 copy-start.3
  110.6 1.0 copy-start.7

commit v3 on v0

v3 whole, which is shorter than its diff:
```python
import jax
import jax.numpy as jnp
from jax import lax
from jax.experimental import pallas as pl
from jax.experimental.pallas import tpu as pltpu
from jax.sharding import PartitionSpec as P

ROWS = 8192
COLS = 26624
RANK = 128
HIGH = lax.Precision.HIGHEST
F32 = jnp.float32
BF16 = jnp.bfloat16

C = 832
R = 1024
DEEP = ((0, 64), (64, 320), (320, 576), (576, 832))
EVEN = tuple((n, n + 208) for n in range(0, C, 208))
BLOCK = 64

QUARTER = C // 4
PART = QUARTER + RANK // 2

CORE, NEAR, FAR = 1, 2, 6


def dot(first, second, dims=((1,), (0,)), precision=None):
    return lax.dot_general(first, second, (dims, ((), ())), precision=precision, preferred_element_type=F32)


def split(x):
    high = x.astype(BF16)
    return high, (x - high.astype(F32)).astype(BF16)


WHOLE = pl.BlockSpec(memory_space=pltpu.VMEM)
ANY = pl.BlockSpec(memory_space=pl.ANY)


def near(*arrays):
    return [pltpu.with_memory_space_constraint(x, pltpu.VMEM) for x in arrays]


def far(*arrays):
    return [pltpu.with_memory_space_constraint(x, pltpu.HBM) for x in arrays]


def params(mib):
    return pltpu.CompilerParams(vmem_limit_bytes=mib << 20)


def start_loads(sources, targets, groups, sems):
    copies = []
    for n, (start, stop) in enumerate(groups):
        rows = pl.ds(start, stop - start)
        pair = [
            pltpu.make_async_copy(source.at[rows], target.at[rows], sems.at[n, k])
            for k, (source, target) in enumerate(zip(sources, targets))
        ]
        for copy in pair:
            copy.start()
        copies.append(pair)
    return copies


def left_kernel(m_hbm, g_hbm, r_hbm, left_ref, m_ref, g_ref, r_ref, both_ref, sum_ref, sems, r_sem):
    first = pltpu.make_async_copy(r_hbm, r_ref, r_sem)
    first.start()
    loads = start_loads((m_hbm, g_hbm), (m_ref, g_ref), DEEP, sems)
    first.wait()
    high, low = split(r_ref[...].T)
    both_ref[:RANK] = high
    both_ref[RANK:] = low
    for n, (start, stop) in enumerate(DEEP):
        for copy in loads[n]:
            copy.wait()
        high, low = split(m_ref[start:stop] + g_ref[start:stop].astype(F32))
        wide = dot(both_ref[:, start:stop], high)
        part = wide[:RANK] + wide[RANK:] + dot(both_ref[:RANK, start:stop], low)
        sum_ref[...] = part if n == 0 else sum_ref[...] + part
    left_ref[...] = sum_ref[...].T


def left_of(m, g, r):
    return pl.pallas_call(
        left_kernel,
        in_specs=[ANY, ANY, ANY],
        out_specs=WHOLE,
        out_shape=pltpu.VMEM((R, RANK), F32),
        scratch_shapes=[
            pltpu.VMEM((C, R), F32),
            pltpu.VMEM((C, R), BF16),
            pltpu.VMEM((C, RANK), F32),
            pltpu.VMEM((2 * RANK, C), BF16),
            pltpu.VMEM((RANK, R), F32),
            pltpu.SemaphoreType.DMA((len(DEEP), 2)),
            pltpu.SemaphoreType.DMA,
        ],
        compiler_params=params(14),
        cost_estimate=pl.CostEstimate(flops=6 * R * C * RANK, bytes_accessed=R * C * 6, transcendentals=0),
        name="left_part",
    )(*far(m, g, r))


def spread_kernel(parts_ref, out_ref, token_ref):
    total = jnp.sum(parts_ref[...], axis=0, keepdims=True)
    out_ref[...] = jnp.broadcast_to(total, out_ref.shape)
    token_ref[...] = total[0, :8]


def sum_and_spread(parts):
    return pl.pallas_call(
        spread_kernel,
        out_shape=[pltpu.VMEM(parts.shape, F32), pltpu.VMEM((8, RANK), F32)],
        in_specs=[WHOLE],
        out_specs=[WHOLE, WHOLE],
        compiler_params=params(4),
        cost_estimate=pl.CostEstimate(flops=parts.size, bytes_accessed=8 * parts.size, transcendentals=0),
        name="sum_and_spread",
    )(*near(parts))


def split_kernel(m_hbm, g_hbm, token_ref, out_ref, m_ref, g_ref, sems):
    loads = start_loads((m_hbm, g_hbm), (m_ref, g_ref), EVEN, sems)
    for n, (start, stop) in enumerate(EVEN):
        for copy in loads[n]:
            copy.wait()
        high, low = split(m_ref[start:stop] + g_ref[start:stop].astype(F32))
        out_ref[start:stop] = high
        out_ref[C + start : C + stop] = low


def split_of(m, g, token):
    return pl.pallas_call(
        split_kernel,
        in_specs=[ANY, ANY, WHOLE],
        out_specs=WHOLE,
        out_shape=pltpu.VMEM((2 * C, R), BF16),
        scratch_shapes=[
            pltpu.VMEM((C, R), F32),
            pltpu.VMEM((C, R), BF16),
            pltpu.SemaphoreType.DMA((len(EVEN), 2)),
        ],
        compiler_params=params(8),
        cost_estimate=pl.CostEstimate(flops=4 * R * C, bytes_accessed=R * C * 10, transcendentals=0),
        name="split_blend",
    )(*far(m, g), *near(token))


def weighted_kernel(core_ref, left_ref, blend_ref, give_ref, first_ref, second_ref, both_ref):
    left = left_ref[...]
    high, low = split(left)
    both_ref[:, :RANK] = high
    both_ref[:, RANK:] = low
    rest = (left - high.astype(F32) - low.astype(F32)).astype(BF16)
    wide = dot(high, both_ref[...], ((0,), (0,)))
    mixed = wide[:, RANK:] + dot(high, rest, ((0,), (0,)))
    gram = wide[:, :RANK] + (mixed + mixed.T + dot(low, low, ((0,), (0,))))
    half = RANK // 2
    give_ref[QUARTER:PART] = gram[:half]
    give_ref[PART + QUARTER :] = gram[half:]
    first_ref[QUARTER:] = gram[:half]
    second_ref[QUARTER:] = gram[half:]
    mine, theirs = core_ref[0] * (C // 2), (1 - core_ref[0]) * (C // 2)

    def product(start):
        wide = dot(blend_ref[pl.ds(pl.multiple_of(start, 16), QUARTER)], both_ref[...])
        rest = dot(blend_ref[pl.ds(pl.multiple_of(C + start, 16), QUARTER)], both_ref[:, :RANK])
        return wide[:, :RANK] + wide[:, RANK:] + rest

    give_ref[:QUARTER] = product(theirs)
    give_ref[PART : PART + QUARTER] = product(theirs + QUARTER)
    first_ref[:QUARTER] = product(mine)
    second_ref[:QUARTER] = product(mine + QUARTER)


def weighted_of(core, left, blend):
    return pl.pallas_call(
        weighted_kernel,
        in_specs=[pl.BlockSpec(memory_space=pltpu.SMEM), WHOLE, WHOLE],
        out_specs=[WHOLE, WHOLE, WHOLE],
        out_shape=[pltpu.VMEM((2 * PART, RANK), F32)] + [pltpu.VMEM((PART, RANK), F32)] * 2,
        scratch_shapes=[pltpu.VMEM((R, 2 * RANK), BF16)],
        compiler_params=params(6),
        cost_estimate=pl.CostEstimate(flops=6 * R * C * RANK, bytes_accessed=R * C * 4, transcendentals=0),
        name="weighted_part",
    )(core, *near(left, blend))


def inverse_kernel(first_ref, second_ref, out_ref, work_ref):
    n, b, t = RANK, BLOCK, 8
    row = lax.broadcasted_iota(jnp.int32, (n, n), 0)
    column = lax.broadcasted_iota(jnp.int32, (n, n), 1)
    work_ref[: n // 2, :n] = first_ref[QUARTER:]
    work_ref[n // 2 :, :n] = second_ref[QUARTER:]
    work_ref[:, n:] = jnp.where(row == column, 1.0, 0.0)
    place = lax.broadcasted_iota(jnp.int32, (t, n), 0)
    for o in range(0, n, b):
        upper = [work_ref[o + k : o + k + t, :n] for k in range(0, b, t)]
        inverse = [work_ref[o + k : o + k + t, n:] for k in range(0, b, t)]
        pivots = []
        for k in range(b // t):
            below = range(k, b // t)
            at = o + k * t
            columns = {q: [jnp.broadcast_to(upper[q][:, at + j : at + j + 1], (t, n)) for j in range(t)] for q in below}
            held = jnp.zeros((t, n), F32)
            for i in range(t):
                pivot = 1.0 / jnp.broadcast_to(columns[k][i][i : i + 1], (t, n))
                held = jnp.where(place == i, pivot, held)
                line = [columns[k][j][i : i + 1] for j in range(t)]
                upper_line, inverse_line = upper[k][i : i + 1], inverse[k][i : i + 1]
                for q in below:
                    factor = columns[q][i] * pivot
                    if q == k:
                        factor = jnp.where(place > i, factor, 0.0)
                    for j in range(i + 1, t):
                        columns[q][j] = columns[q][j] - factor * line[j]
                    upper[q] = upper[q] - factor * upper_line
                    inverse[q] = inverse[q] - factor * inverse_line
            pivots.append(held)
        root = jnp.sqrt(jnp.concatenate(pivots, axis=0))
        upper_block = jnp.concatenate(upper, axis=0) * root
        inverse_block = jnp.concatenate(inverse, axis=0) * root
        out_ref[o : o + b] = inverse_block
        if o + b < n:
            done = jnp.concatenate([upper_block, inverse_block], axis=1)
            work_ref[o + b :] -= dot(upper_block[:, o + b :], done, ((0,), (0,)), HIGH)


def inverse_of(first, second):
    return pl.pallas_call(
        inverse_kernel,
        out_shape=pltpu.VMEM((RANK, RANK), F32),
        in_specs=[WHOLE, WHOLE],
        out_specs=WHOLE,
        scratch_shapes=[pltpu.VMEM((RANK, 2 * RANK), F32)],
        compiler_params=params(2),
        cost_estimate=pl.CostEstimate(flops=60 << 30, bytes_accessed=1 << 17, transcendentals=0),
        name="inverse_factor",
    )(*near(first, second))


def across_kernel(core_ref, first_ref, second_ref, other_ref, inverse_ref, across_ref, colsq_ref):
    high, low = split(inverse_ref[...].T)
    three = jnp.concatenate([high, high, low], axis=0)
    mine, theirs = core_ref[0] * (C // 2), (1 - core_ref[0]) * (C // 2)
    total = jnp.zeros((1, RANK), F32)
    for part, start in (
        (first_ref[:QUARTER], mine),
        (second_ref[:QUARTER], mine + QUARTER),
        (other_ref[...], theirs),
    ):
        high, low = split(part)
        part = dot(jnp.concatenate([high, low, high], axis=1), three)
        across_ref[pl.ds(pl.multiple_of(start, 8), part.shape[0])] = part
        total = total + jnp.sum(part * part, axis=0, keepdims=True)
    colsq_ref[...] = jnp.broadcast_to(total, colsq_ref.shape)


def across_of(core, first, second, other, inverse):
    return pl.pallas_call(
        across_kernel,
        in_specs=[pl.BlockSpec(memory_space=pltpu.SMEM), WHOLE, WHOLE, WHOLE, WHOLE],
        out_specs=[WHOLE, WHOLE],
        out_shape=[pltpu.VMEM((C, RANK), F32), pltpu.VMEM((32, RANK), F32)],
        compiler_params=params(4),
        cost_estimate=pl.CostEstimate(flops=12 * C * RANK * RANK, bytes_accessed=C * RANK * 8, transcendentals=0),
        name="across_part",
    )(core, *near(first, second, other, inverse))


def store(source, target, groups, sems, n):
    rows = pl.ds(groups[n][0], groups[n][1] - groups[n][0])
    copy = pltpu.make_async_copy(source.at[rows], target.at[rows], sems.at[n])
    copy.start()
    return copy


def momentum_kernel(m_hbm, g_hbm, left_ref, inverse_ref, across_ref, new_hbm, basis_ref, m_ref, g_ref, new_ref, sems, out_sems):
    loads = start_loads((m_hbm, g_hbm), (m_ref, g_ref), EVEN, sems)
    high, low = split(dot(inverse_ref[...], left_ref[...], ((1,), (1,)), HIGH))
    basis_ref[:RANK] = high
    basis_ref[RANK : 2 * RANK] = high
    basis_ref[2 * RANK :] = low
    stores = []
    for n, (start, stop) in enumerate(EVEN):
        for copy in loads[n]:
            copy.wait()
        wide = jnp.concatenate(split(across_ref[start:stop] * 0.05), axis=1)
        blend = m_ref[start:stop] + g_ref[start:stop].astype(F32)
        new_ref[start:stop] = blend - dot(wide, basis_ref[: 2 * RANK])
        stores.append(store(new_ref, new_hbm, EVEN, out_sems, n))
    for copy in stores:
        copy.wait()


def momentum_of(m, g, left, inverse, across):
    return pl.pallas_call(
        momentum_kernel,
        in_specs=[ANY, ANY, WHOLE, WHOLE, WHOLE],
        out_specs=[ANY, WHOLE],
        out_shape=[pltpu.HBM((C, R), F32), pltpu.VMEM((3 * RANK, R), BF16)],
        scratch_shapes=[
            pltpu.VMEM((C, R), F32),
            pltpu.VMEM((C, R), BF16),
            pltpu.VMEM((C, R), F32),
            pltpu.SemaphoreType.DMA((len(EVEN), 2)),
            pltpu.SemaphoreType.DMA((len(EVEN),)),
        ],
        compiler_params=params(14),
        cost_estimate=pl.CostEstimate(flops=4 * R * C * RANK, bytes_accessed=R * C * 10, transcendentals=0),
        name="new_momentum",
    )(*far(m, g), *near(left, inverse, across))


def update_kernel(across_ref, colsq_ref, basis_ref, update_hbm, update_ref, sems):
    colsq = jnp.sum(colsq_ref[...], axis=0, keepdims=True)
    scale = (ROWS * COLS / RANK) ** 0.5 / jnp.sqrt(colsq + 1e-06)
    stores = []
    for n, (start, stop) in enumerate(EVEN):
        high, low = split(across_ref[start:stop] * scale)
        product = dot(jnp.concatenate([high, low, high], axis=1), basis_ref[...])
        update_ref[start:stop] = product.astype(BF16)
        stores.append(store(update_ref, update_hbm, EVEN, sems, n))
    for copy in stores:
        copy.wait()


def update_of(across, colsq, basis):
    return pl.pallas_call(
        update_kernel,
        in_specs=[WHOLE, WHOLE, WHOLE],
        out_specs=ANY,
        out_shape=pltpu.HBM((C, R), BF16),
        scratch_shapes=[pltpu.VMEM((C, R), BF16), pltpu.SemaphoreType.DMA((len(EVEN),))],
        compiler_params=params(6),
        cost_estimate=pl.CostEstimate(flops=6 * R * C * RANK, bytes_accessed=R * C * 2, transcendentals=0),
        name="update",
    )(*near(across, colsq, basis))


def exchange(blocks, axis):
    return lax.all_to_all(blocks, axis, 0, 0)


def swap(x, flip):
    return lax.ppermute(x, "row", [(i, i ^ flip) for i in range(8)])


def body(momentum, gradient, right_factor):
    m, g = momentum.T, gradient.T
    core = lax.rem(lax.axis_index("row"), 2).astype(jnp.int32).reshape(1)
    partial = left_of(m, g, right_factor)
    parts = exchange(partial.reshape(32, R // 32, RANK), "col")
    spread, token = sum_and_spread(parts)
    left = exchange(spread, "col").reshape(R, RANK)
    blend = split_of(m, g, token)

    give, first, second = weighted_of(core, left, blend)
    given = swap(give, CORE)
    first, second = first + given[:PART], second + given[PART:]
    first, second = first + swap(first, NEAR), second + swap(second, FAR)
    first, second = first + swap(first, FAR), second + swap(second, NEAR)
    other = swap(jnp.concatenate([first[:QUARTER], second[:QUARTER]], axis=0), CORE)
    inverse = inverse_of(first, second)

    across, colsq = across_of(core, first, second, other, inverse)
    colsq = exchange(colsq.reshape(32, 1, RANK), "col").reshape(32, RANK)
    new_momentum, basis = momentum_of(m, g, left, inverse, across)
    update = update_of(across, colsq, basis)
    return (new_momentum.T, update.T)


def solution(mesh):
    in_specs = (P("row", "col"), P("row", "col"), P("col", None))
    out_specs = (P("row", "col"), P("row", "col"))
    return jax.shard_map(body, mesh=mesh, in_specs=in_specs, out_specs=out_specs, check_vma=False)
```

time: 421 us -> 97.2 us (0.23)
  the two profiles are of different devices: /device:TPU:0 before, /device:TPU:1 now
where the time goes in v3:
time: 97.2 us; the launch traced here: 96.8 us
  blocking collectives  26 us (27%)
  starting transfers between devices  24.7 us (25%)
  waiting for transfers between devices  23.8 us (24%)
  Pallas kernels  21.5 us (22%)
    all_to_all x1, blocking collectives, exchange(): return lax.all_to_all(blocks, axis, 0, 0)  26 us
    all_to_all x2, waiting for transfers between devices, exchange(): return lax.all_to_all(blocks, axis, 0, 0)  14.7 us
    all_to_all x2, starting transfers between devices, exchange(): return lax.all_to_all(blocks, axis, 0, 0)  12.6 us
    ppermute x6, starting transfers between devices, swap(): return lax.ppermute(x, 'row', [(i, i ^ flip) for i in range(8)])  12.1 us
    ppermute x6, waiting for transfers between devices, swap(): return lax.ppermute(x, 'row', [(i, i ^ flip) for i in range(8)])  9.03 us
    pallas_call x1, Pallas kernels, momentum_of(): pl.pallas_call(momentum_kernel, in_specs=[ANY, ANY, WHOLE, WHOLE, WHOLE],...  4.76 us
    pallas_call x1, Pallas kernels, left_of(): pl.pallas_call(left_kernel, in_specs=[ANY, ANY, ANY], out_specs=WHOLE, ou...  4.12 us
    pallas_call x1, Pallas kernels, inverse_of(): pl.pallas_call(inverse_kernel, out_shape=pltpu.VMEM((RANK, RANK), F32), i...  3.8 us
  transfers between devices with their start and end apart: 8, of which 7 were waited for; matrix products, arithmetic and copies ran while one was open for 0% of the time, Pallas kernels for 12%

profile of v3, /device:TPU:1, one launch (start us, length us, event | category | flops | bytes accessed | tf_op | source)
XLA Modules:
  0.0 96.8 jit_solution(2455917770299243517)
XLA Ops:
  0.6 4.1 %left_part.1 = f32[1024,128]{1,0:T(8,128)S(1)} custom-call(f32[832,1024]{1,0:T(8,128)} %bitcast.13, bf16[832,1024]{1,0:T(8,128)(2,1)} %bitcast.16, f32[832,128]{1,0:T(8,128)} %r_hbm.1), custom_call_target="tpu_custom_call" | custom-call | flops 654311424 | bytes 5111808 | tf_op jit(solution)/shard_map/left_part/pallas_call | solution.py:85
  4.8 26.0 %all_to_all.15.parts_ref = f32[32,32,128]{2,1,0:T(8,128)S(1)} all-to-all(f32[32,32,128]{2,1,0:T(8,128)S(1)} %bitcast.11), channel_id=1, replica_groups=mesh['row'=8,'col'=32] {'col'}, dimensions={0} | all-to-all | bytes 1048576 | tf_op jit(solution)/shard_map/all_to_all | solution.py:343
  30.7 0.9 sum_and_spread.1
  31.6 7.6 %all-to-all-start.1 = ((f32[32,32,128]{2,1,0:T(8,128)}), f32[32,32,128]{2,1,0:T(8,128)}, u32[]{:S(2)}, u32[]{:S(2)}) async-start(f32[32,32,128]{2,1,0:T(8,128)} %get-tuple-element.11), calls=%async_computation.1 | async-start | bytes 1048576 | tf_op jit(solution)/shard_map/all_to_all | solution.py:343
  39.2 2.7 %split_blend.1.blend_ref = bf16[1664,1024]{1,0:T(8,128)(2,1)S(1)} custom-call(f32[832,1024]{1,0:T(8,128)} %bitcast.14, bf16[832,1024]{1,0:T(8,128)(2,1)} %bitcast.17, f32[8,128]{1,0:T(8,128)S(1)} %get-tuple-element.12.token_ref), custom_call_target="tpu_custom_call" | custom-call | flops 3407872 | bytes 8519680 | tf_op jit(solution)/shard_map/split_blend/pallas_call | solution.py:134
  41.9 10.9 %all-to-all-done.1 = f32[32,32,128]{2,1,0:T(8,128)} async-done(((f32[32,32,128]{2,1,0:T(8,128)}), f32[32,32,128]{2,1,0:T(8,128)}, u32[]{:S(2)}, u32[]{:S(2)}) %all-to-all-start.1) | async-done | bytes 524320 | tf_op jit(solution)/shard_map/all_to_all | solution.py:343
  52.8 2.4 %weighted_part.1 = (f32[544,128]{1,0:T(8,128)S(1)}, f32[272,128]{1,0:T(8,128)S(1)}, f32[272,128]{1,0:T(8,128)S(1)}) custom-call(s32[1]{0:T(128)} %bitcast.4.core_ref, f32[1024,128]{1,0:T(8,128)} %bitcast.3.left_ref, bf16[1664,1024]{1,0:T(8,128)(2,1)S(1)} %split_blend.1.blend_ref), custom_call_target="tpu_custom_call" | custom-call | flops 654311424 | bytes 3407872 | tf_op jit(solution)/shard_map/weighted_part/pallas_call | solution.py:178
  55.2 4.6 %collective-permute-start = (f32[544,128]{1,0:T(8,128)S(1)}, f32[544,128]{1,0:T(8,128)S(1)}, u32[]{:S(2)}, u32[]{:S(2)}) collective-permute-start(f32[544,128]{1,0:T(8,128)S(1)} %get-tuple-element.14), channel_id=1, source_target_pairs={{0,32},{32,0},{64,96},{96,64},{128,160},{160,128},{192,224},{224,1... | collective-permute-start | bytes 835592 | tf_op jit(solution)/shard_map/ppermute | solution.py:347
  59.9 1.2 %collective-permute-done = f32[544,128]{1,0:T(8,128)S(1)} collective-permute-done((f32[544,128]{1,0:T(8,128)S(1)}, f32[544,128]{1,0:T(8,128)S(1)}, u32[]{:S(2)}, u32[]{:S(2)}) %collective-permute-start) | collective-permute-done | bytes 278560 | tf_op jit(solution)/shard_map/ppermute | solution.py:347
  61.1 2.8 %collective-permute-start.3 = (f32[272,128]{1,0:T(8,128)S(1)}, f32[272,128]{1,0:T(8,128)S(1)}, u32[]{:S(2)}, u32[]{:S(2)}) collective-permute-start(f32[272,128]{1,0:T(8,128)S(1)} %get-tuple-element.20), channel_id=1, source_target_pairs={{0,192},{32,224},{64,128},{96,160},{128,64},{160,96},{192,0},{224,... | collective-permute-start | bytes 417800 | tf_op jit(solution)/shard_map/ppermute | solution.py:347
  63.9 3.5 %collective-permute-done.3 = f32[272,128]{1,0:T(8,128)S(1)} collective-permute-done((f32[272,128]{1,0:T(8,128)S(1)}, f32[272,128]{1,0:T(8,128)S(1)}, u32[]{:S(2)}, u32[]{:S(2)}) %collective-permute-start.3) | collective-permute-done | bytes 139296 | tf_op jit(solution)/shard_map/ppermute | solution.py:347
  67.4 0.1 collective-permute-start.4
  67.5 1.0 collective-permute-done.1
  68.5 1.8 %collective-permute-start.2 = (f32[272,128]{1,0:T(8,128)S(1)}, f32[272,128]{1,0:T(8,128)S(1)}, u32[]{:S(2)}, u32[]{:S(2)}) collective-permute-start(f32[272,128]{1,0:T(8,128)S(1)} %add.19), channel_id=1, source_target_pairs={{0,192},{32,224},{64,128},{96,160},{128,64},{160,96},{192,0},{224,... | collective-permute-start | bytes 417800 | tf_op jit(solution)/shard_map/ppermute | solution.py:347
  70.2 1.2 %collective-permute-done.4 = f32[272,128]{1,0:T(8,128)S(1)} collective-permute-done((f32[272,128]{1,0:T(8,128)S(1)}, f32[272,128]{1,0:T(8,128)S(1)}, u32[]{:S(2)}, u32[]{:S(2)}) %collective-permute-start.4) | collective-permute-done | bytes 139296 | tf_op jit(solution)/shard_map/ppermute | solution.py:347
  71.4 2.2 %collective-permute-done.2 = f32[272,128]{1,0:T(8,128)S(1)} collective-permute-done((f32[272,128]{1,0:T(8,128)S(1)}, f32[272,128]{1,0:T(8,128)S(1)}, u32[]{:S(2)}, u32[]{:S(2)}) %collective-permute-start.2) | collective-permute-done | bytes 139296 | tf_op jit(solution)/shard_map/ppermute | solution.py:347
  73.7 2.8 %collective-permute-start.5 = (f32[416,128]{1,0:T(8,128)S(1)}, f32[416,128]{1,0:T(8,128)S(1)}, u32[]{:S(2)}, u32[]{:S(2)}) collective-permute-start(f32[416,128]{1,0:T(8,128)S(1)} %pad_maximum_fusion), channel_id=1, source_target_pairs={{0,32},{32,0},{64,96},{96,64},{128,160},{160,128},{192,224},{224,1... | collective-permute-start | bytes 638984 | tf_op jit(solution)/shard_map/ppermute | solution.py:347
  76.5 3.8 %inverse_factor.1.inverse_ref = f32[128,128]{1,0:T(8,128)S(1)} custom-call(f32[272,128]{1,0:T(8,128)S(1)} %add.20.first_ref, f32[272,128]{1,0:T(8,128)S(1)} %add.23.second_ref), custom_call_target="tpu_custom_call" | custom-call | flops 64424509440 | bytes 131072 | tf_op jit(solution)/shard_map/inverse_factor/pallas_call | solution.py:231
  80.3 0.0 collective-permute-done.5.other_ref
  80.3 1.1 %across_part.1 = (f32[832,128]{1,0:T(8,128)S(1)}, f32[32,128]{1,0:T(8,128)}) custom-call(s32[1]{0:T(128)} %bitcast.4.core_ref, f32[272,128]{1,0:T(8,128)S(1)} %add.20.first_ref, f32[272,128]{1,0:T(8,128)S(1)} %add.23.second_ref, f32[416,128]{1,0:T(8,128)S(1)} %collective-permute-done.5.other_ref, f32[128,128]{1,0:T(8,128)S(1)} %inverse_factor.1.inverse_ref), custom_call_target="tpu_custom_call" | custom-call | flops 163577856 | bytes 851968 | tf_op jit(solution)/shard_map/across_part/pallas_call | solution.py:261
  81.4 5.0 %all-to-all-start.2 = ((f32[32,1,128]{2,1,0:T(1,128)}), f32[32,1,128]{2,1,0:T(1,128)S(1)}, u32[]{:S(2)}, u32[]{:S(2)}) async-start(f32[32,1,128]{2,1,0:T(1,128)} %bitcast.7), calls=%async_computation.2 | async-start | bytes 32768 | tf_op jit(solution)/shard_map/all_to_all | solution.py:343
  86.4 4.8 %new_momentum.1 = (f32[832,1024]{1,0:T(8,128)}, bf16[384,1024]{1,0:T(8,128)(2,1)S(1)}) custom-call(f32[832,1024]{1,0:T(8,128)} %bitcast.15, bf16[832,1024]{1,0:T(8,128)(2,1)} %bitcast.18, f32[1024,128]{1,0:T(8,128)} %bitcast.3.left_ref, f32[128,128]{1,0:T(8,128)S(1)} %inverse_factor.1.inverse_ref, f32[832,128]{1,0:T(8,128)S(1)} %get-tuple-element.16.across_ref), custom_call_target="tpu_custom_call" | custom-call | flops 436207616 | bytes 8519680 | tf_op jit(solution)/shard_map/new_momentum/pallas_call | solution.py:298
  91.1 3.8 %all-to-all-done.2 = f32[32,1,128]{2,1,0:T(1,128)S(1)} async-done(((f32[32,1,128]{2,1,0:T(1,128)}), f32[32,1,128]{2,1,0:T(1,128)S(1)}, u32[]{:S(2)}, u32[]{:S(2)}) %all-to-all-start.2) | async-done | bytes 16416 | tf_op jit(solution)/shard_map/all_to_all | solution.py:343
  94.9 1.9 %update.1 = bf16[832,1024]{1,0:T(8,128)(2,1)} custom-call(f32[832,128]{1,0:T(8,128)S(1)} %get-tuple-element.16.across_ref, f32[32,128]{1,0:T(8,128)S(1)} %bitcast.12, bf16[384,1024]{1,0:T(8,128)(2,1)S(1)} %get-tuple-element.19.basis_ref), custom_call_target="tpu_custom_call" | custom-call | flops 654311424 | bytes 1703936 | tf_op jit(solution)/shard_map/update/pallas_call | solution.py:330
  (9 shorter events, 0.2 us)
Async XLA Ops:
  31.6 21.2 %all-to-all-start.1 = ((f32[32,32,128]{2,1,0:T(8,128)}), f32[32,32,128]{2,1,0:T(8,128)}, u32[]{:S(2)}, u32[]{:S(2)}) async-start(f32[32,32,128]{2,1,0:T(8,128)} %get-tuple-element.11), calls=%async_computation.1 | async-start | bytes 1048576 | tf_op jit(solution)/shard_map/all_to_all | solution.py:343
  55.2 5.8 %collective-permute-start = (f32[544,128]{1,0:T(8,128)S(1)}, f32[544,128]{1,0:T(8,128)S(1)}, u32[]{:S(2)}, u32[]{:S(2)}) collective-permute-start(f32[544,128]{1,0:T(8,128)S(1)} %get-tuple-element.14), channel_id=1, source_target_pairs={{0,32},{32,0},{64,96},{96,64},{128,160},{160,128},{192,224},{224,1... | collective-permute-start | bytes 835592 | tf_op jit(solution)/shard_map/ppermute | solution.py:347
  61.1 6.3 %collective-permute-start.3 = (f32[272,128]{1,0:T(8,128)S(1)}, f32[272,128]{1,0:T(8,128)S(1)}, u32[]{:S(2)}, u32[]{:S(2)}) collective-permute-start(f32[272,128]{1,0:T(8,128)S(1)} %get-tuple-element.20), channel_id=1, source_target_pairs={{0,192},{32,224},{64,128},{96,160},{128,64},{160,96},{192,0},{224,... | collective-permute-start | bytes 417800 | tf_op jit(solution)/shard_map/ppermute | solution.py:347
  63.9 4.6 %collective-permute-start.1 = (f32[272,128]{1,0:T(8,128)S(1)}, f32[272,128]{1,0:T(8,128)S(1)}, u32[]{:S(2)}, u32[]{:S(2)}) collective-permute-start(f32[272,128]{1,0:T(8,128)S(1)} %get-tuple-element.21), channel_id=1, source_target_pairs={{0,64},{32,96},{64,0},{96,32},{128,192},{160,224},{192,128},{224,1... | collective-permute-start | bytes 417800 | tf_op jit(solution)/shard_map/ppermute | solution.py:347
  67.4 4.0 %collective-permute-start.4 = (f32[272,128]{1,0:T(8,128)S(1)}, f32[272,128]{1,0:T(8,128)S(1)}, u32[]{:S(2)}, u32[]{:S(2)}) collective-permute-start(f32[272,128]{1,0:T(8,128)S(1)} %add.22), channel_id=1, source_target_pairs={{0,64},{32,96},{64,0},{96,32},{128,192},{160,224},{192,128},{224,1... | collective-permute-start | bytes 417800 | tf_op jit(solution)/shard_map/ppermute | solution.py:347
  68.5 5.2 %collective-permute-start.2 = (f32[272,128]{1,0:T(8,128)S(1)}, f32[272,128]{1,0:T(8,128)S(1)}, u32[]{:S(2)}, u32[]{:S(2)}) collective-permute-start(f32[272,128]{1,0:T(8,128)S(1)} %add.19), channel_id=1, source_target_pairs={{0,192},{32,224},{64,128},{96,160},{128,64},{160,96},{192,0},{224,... | collective-permute-start | bytes 417800 | tf_op jit(solution)/shard_map/ppermute | solution.py:347
  73.7 6.6 %collective-permute-start.5 = (f32[416,128]{1,0:T(8,128)S(1)}, f32[416,128]{1,0:T(8,128)S(1)}, u32[]{:S(2)}, u32[]{:S(2)}) collective-permute-start(f32[416,128]{1,0:T(8,128)S(1)} %pad_maximum_fusion), channel_id=1, source_target_pairs={{0,32},{32,0},{64,96},{96,64},{128,160},{160,128},{192,224},{224,1... | collective-permute-start | bytes 638984 | tf_op jit(solution)/shard_map/ppermute | solution.py:347
  81.4 13.6 %all-to-all-start.2 = ((f32[32,1,128]{2,1,0:T(1,128)}), f32[32,1,128]{2,1,0:T(1,128)S(1)}, u32[]{:S(2)}, u32[]{:S(2)}) async-start(f32[32,1,128]{2,1,0:T(1,128)} %bitcast.7), calls=%async_computation.2 | async-start | bytes 32768 | tf_op jit(solution)/shard_map/all_to_all | solution.py:343

commit v4 on v3

--- a/solution.py
+++ b/solution.py
@@ -18,10 +18,8 @@
 EVEN = tuple((n, n + 208) for n in range(0, C, 208))
 BLOCK = 64
 
-QUARTER = C // 4
-PART = QUARTER + RANK // 2
-
-CORE, NEAR, FAR = 1, 2, 6
+HALF = C // 2
+SMEM = pl.BlockSpec(memory_space=pltpu.SMEM)
 
 
 def dot(first, second, dims=((1,), (0,)), precision=None):
@@ -147,39 +145,32 @@
     )(*far(m, g), *near(token))
 
 
-def weighted_kernel(core_ref, left_ref, blend_ref, give_ref, first_ref, second_ref, both_ref):
+def weighted_kernel(core_ref, left_ref, blend_ref, give_ref, keep_ref, both_ref):
     left = left_ref[...]
     high, low = split(left)
+    rest = (left - high.astype(F32) - low.astype(F32)).astype(BF16)
     both_ref[:, :RANK] = high
     both_ref[:, RANK:] = low
-    rest = (left - high.astype(F32) - low.astype(F32)).astype(BF16)
     wide = dot(high, both_ref[...], ((0,), (0,)))
     mixed = wide[:, RANK:] + dot(high, rest, ((0,), (0,)))
     gram = wide[:, :RANK] + (mixed + mixed.T + dot(low, low, ((0,), (0,))))
-    half = RANK // 2
-    give_ref[QUARTER:PART] = gram[:half]
-    give_ref[PART + QUARTER :] = gram[half:]
-    first_ref[QUARTER:] = gram[:half]
-    second_ref[QUARTER:] = gram[half:]
-    mine, theirs = core_ref[0] * (C // 2), (1 - core_ref[0]) * (C // 2)
-
-    def product(start):
-        wide = dot(blend_ref[pl.ds(pl.multiple_of(start, 16), QUARTER)], both_ref[...])
-        rest = dot(blend_ref[pl.ds(pl.multiple_of(C + start, 16), QUARTER)], both_ref[:, :RANK])
-        return wide[:, :RANK] + wide[:, RANK:] + rest
-
-    give_ref[:QUARTER] = product(theirs)
-    give_ref[PART : PART + QUARTER] = product(theirs + QUARTER)
-    first_ref[:QUARTER] = product(mine)
-    second_ref[:QUARTER] = product(mine + QUARTER)
+    give_ref[HALF:] = gram
+    keep_ref[HALF:] = gram
+    core = core_ref[0]
+    for out_ref, base in ((give_ref, HALF - core * HALF), (keep_ref, core * HALF)):
+        for step in range(0, HALF, HALF // 2):
+            high = blend_ref[pl.ds(pl.multiple_of(base + step, 16), HALF // 2)]
+            low = blend_ref[pl.ds(pl.multiple_of(base + C + step, 16), HALF // 2)]
+            wide = dot(high, both_ref[...])
+            out_ref[step : step + HALF // 2] = wide[:, :RANK] + wide[:, RANK:] + dot(low, both_ref[:, :RANK])
 
 
 def weighted_of(core, left, blend):
     return pl.pallas_call(
         weighted_kernel,
-        in_specs=[pl.BlockSpec(memory_space=pltpu.SMEM), WHOLE, WHOLE],
-        out_specs=[WHOLE, WHOLE, WHOLE],
-        out_shape=[pltpu.VMEM((2 * PART, RANK), F32)] + [pltpu.VMEM((PART, RANK), F32)] * 2,
+        in_specs=[SMEM, WHOLE, WHOLE],
+        out_specs=[WHOLE, WHOLE],
+        out_shape=[pltpu.VMEM((HALF + RANK, RANK), F32)] * 2,
         scratch_shapes=[pltpu.VMEM((R, 2 * RANK), BF16)],
         compiler_params=params(6),
         cost_estimate=pl.CostEstimate(flops=6 * R * C * RANK, bytes_accessed=R * C * 4, transcendentals=0),
@@ -187,12 +178,11 @@
     )(core, *near(left, blend))
 
 
-def inverse_kernel(first_ref, second_ref, out_ref, work_ref):
+def inverse_kernel(gram_ref, out_ref, work_ref):
     n, b, t = RANK, BLOCK, 8
     row = lax.broadcasted_iota(jnp.int32, (n, n), 0)
     column = lax.broadcasted_iota(jnp.int32, (n, n), 1)
-    work_ref[: n // 2, :n] = first_ref[QUARTER:]
-    work_ref[n // 2 :, :n] = second_ref[QUARTER:]
+    work_ref[:, :n] = gram_ref[...]
     work_ref[:, n:] = jnp.where(row == column, 1.0, 0.0)
     place = lax.broadcasted_iota(jnp.int32, (t, n), 0)
     for o in range(0, n, b):
@@ -227,46 +217,38 @@
             work_ref[o + b :] -= dot(upper_block[:, o + b :], done, ((0,), (0,)), HIGH)
 
 
-def inverse_of(first, second):
+def inverse_of(gram):
     return pl.pallas_call(
         inverse_kernel,
         out_shape=pltpu.VMEM((RANK, RANK), F32),
-        in_specs=[WHOLE, WHOLE],
+        in_specs=[WHOLE],
         out_specs=WHOLE,
         scratch_shapes=[pltpu.VMEM((RANK, 2 * RANK), F32)],
         compiler_params=params(2),
         cost_estimate=pl.CostEstimate(flops=60 << 30, bytes_accessed=1 << 17, transcendentals=0),
         name="inverse_factor",
-    )(*near(first, second))
-
-
-def across_kernel(core_ref, first_ref, second_ref, other_ref, inverse_ref, across_ref, colsq_ref):
+    )(*near(gram))
+
+
+def across_kernel(part_ref, got_ref, inverse_ref, across_ref, colsq_ref):
     high, low = split(inverse_ref[...].T)
     three = jnp.concatenate([high, high, low], axis=0)
-    mine, theirs = core_ref[0] * (C // 2), (1 - core_ref[0]) * (C // 2)
-    total = jnp.zeros((1, RANK), F32)
-    for part, start in (
-        (first_ref[:QUARTER], mine),
-        (second_ref[:QUARTER], mine + QUARTER),
-        (other_ref[...], theirs),
-    ):
-        high, low = split(part)
-        part = dot(jnp.concatenate([high, low, high], axis=1), three)
-        across_ref[pl.ds(pl.multiple_of(start, 8), part.shape[0])] = part
-        total = total + jnp.sum(part * part, axis=0, keepdims=True)
-    colsq_ref[...] = jnp.broadcast_to(total, colsq_ref.shape)
-
-
-def across_of(core, first, second, other, inverse):
+    high, low = split(part_ref[...] + got_ref[...])
+    across = dot(jnp.concatenate([high, low, high], axis=1), three)
+    across_ref[...] = across
+    colsq_ref[...] = jnp.broadcast_to(jnp.sum(across * across, axis=0, keepdims=True), colsq_ref.shape)
+
+
+def across_of(part, got, inverse):
     return pl.pallas_call(
         across_kernel,
-        in_specs=[pl.BlockSpec(memory_space=pltpu.SMEM), WHOLE, WHOLE, WHOLE, WHOLE],
+        in_specs=[WHOLE, WHOLE, WHOLE],
         out_specs=[WHOLE, WHOLE],
-        out_shape=[pltpu.VMEM((C, RANK), F32), pltpu.VMEM((32, RANK), F32)],
+        out_shape=[pltpu.VMEM((HALF, RANK), F32), pltpu.VMEM((64, RANK), F32)],
         compiler_params=params(4),
-        cost_estimate=pl.CostEstimate(flops=12 * C * RANK * RANK, bytes_accessed=C * RANK * 8, transcendentals=0),
+        cost_estimate=pl.CostEstimate(flops=6 * C * RANK * RANK, bytes_accessed=C * RANK * 8, transcendentals=0),
         name="across_part",
-    )(core, *near(first, second, other, inverse))
+    )(*near(part, got, inverse))
 
 
 def store(source, target, groups, sems, n):
@@ -276,12 +258,24 @@
     return copy
 
 
-def momentum_kernel(m_hbm, g_hbm, left_ref, inverse_ref, across_ref, new_hbm, basis_ref, m_ref, g_ref, new_ref, sems, out_sems):
+def momentum_kernel(
+    core_ref, m_hbm, g_hbm, left_hbm, inverse_ref, mine_ref, other_ref,
+    new_hbm, basis_ref, across_ref, m_ref, g_ref, left_ref, new_ref, sems, left_sem, out_sems,
+):
+    load = pltpu.make_async_copy(left_hbm, left_ref, left_sem)
+    load.start()
     loads = start_loads((m_hbm, g_hbm), (m_ref, g_ref), EVEN, sems)
-    high, low = split(dot(inverse_ref[...], left_ref[...], ((1,), (1,)), HIGH))
+    high, low = split(inverse_ref[...])
+    load.wait()
+    both = split(left_ref[...])
+    basis = dot(jnp.concatenate([high, high], axis=1), jnp.concatenate(both, axis=1), ((1,), (1,)))
+    high, low = split(basis + dot(low, both[0], ((1,), (1,))))
     basis_ref[:RANK] = high
     basis_ref[RANK : 2 * RANK] = high
     basis_ref[2 * RANK :] = low
+    mine = core_ref[0] * HALF
+    across_ref[pl.ds(pl.multiple_of(mine, 8), HALF)] = mine_ref[...]
+    across_ref[pl.ds(pl.multiple_of(HALF - mine, 8), HALF)] = other_ref[...]
     stores = []
     for n, (start, stop) in enumerate(EVEN):
         for copy in loads[n]:
@@ -294,23 +288,25 @@
         copy.wait()
 
 
-def momentum_of(m, g, left, inverse, across):
+def momentum_of(core, m, g, left, inverse, mine, other):
     return pl.pallas_call(
         momentum_kernel,
-        in_specs=[ANY, ANY, WHOLE, WHOLE, WHOLE],
-        out_specs=[ANY, WHOLE],
-        out_shape=[pltpu.HBM((C, R), F32), pltpu.VMEM((3 * RANK, R), BF16)],
+        in_specs=[SMEM, ANY, ANY, ANY, WHOLE, WHOLE, WHOLE],
+        out_specs=[ANY, WHOLE, WHOLE],
+        out_shape=[pltpu.HBM((C, R), F32), pltpu.VMEM((3 * RANK, R), BF16), pltpu.VMEM((C, RANK), F32)],
         scratch_shapes=[
             pltpu.VMEM((C, R), F32),
             pltpu.VMEM((C, R), BF16),
+            pltpu.VMEM((R, RANK), F32),
             pltpu.VMEM((C, R), F32),
             pltpu.SemaphoreType.DMA((len(EVEN), 2)),
+            pltpu.SemaphoreType.DMA,
             pltpu.SemaphoreType.DMA((len(EVEN),)),
         ],
         compiler_params=params(14),
         cost_estimate=pl.CostEstimate(flops=4 * R * C * RANK, bytes_accessed=R * C * 10, transcendentals=0),
         name="new_momentum",
-    )(*far(m, g), *near(left, inverse, across))
+    )(core, *far(m, g), left, *near(inverse, mine, other))
 
 
 def update_kernel(across_ref, colsq_ref, basis_ref, update_hbm, update_ref, sems):
@@ -339,39 +335,43 @@
     )(*near(across, colsq, basis))
 
 
-def exchange(blocks, axis):
-    return lax.all_to_all(blocks, axis, 0, 0)
-
-
-def swap(x, flip):
-    return lax.ppermute(x, "row", [(i, i ^ flip) for i in range(8)])
+def exchange(blocks, axes):
+    return lax.all_to_all(blocks, axes, 0, 0)
+
+
+def swap_core(block):
+    return lax.ppermute(block, "core", [(0, 1), (1, 0)])
+
+
+def swap_y(block, step):
+    pairs = [(i, i ^ 2 if i % 2 == step else 7 - (i ^ 1)) for i in range(8)]
+    return lax.ppermute(block, ("y", "core"), pairs)
 
 
 def body(momentum, gradient, right_factor):
     m, g = momentum.T, gradient.T
-    core = lax.rem(lax.axis_index("row"), 2).astype(jnp.int32).reshape(1)
+    core = lax.axis_index("core").astype(jnp.int32).reshape(1)
     partial = left_of(m, g, right_factor)
-    parts = exchange(partial.reshape(32, R // 32, RANK), "col")
-    spread, token = sum_and_spread(parts)
-    left = exchange(spread, "col").reshape(R, RANK)
+    spread, token = sum_and_spread(exchange(partial.reshape(32, R // 32, RANK), ("x", "z")))
+    left = exchange(spread, ("x", "z")).reshape(R, RANK)
     blend = split_of(m, g, token)
 
-    give, first, second = weighted_of(core, left, blend)
-    given = swap(give, CORE)
-    first, second = first + given[:PART], second + given[PART:]
-    first, second = first + swap(first, NEAR), second + swap(second, FAR)
-    first, second = first + swap(first, FAR), second + swap(second, NEAR)
-    other = swap(jnp.concatenate([first[:QUARTER], second[:QUARTER]], axis=0), CORE)
-    inverse = inverse_of(first, second)
-
-    across, colsq = across_of(core, first, second, other, inverse)
-    colsq = exchange(colsq.reshape(32, 1, RANK), "col").reshape(32, RANK)
-    new_momentum, basis = momentum_of(m, g, left, inverse, across)
+    give, part = weighted_of(core, left, blend)
+    part = part + swap_core(give)
+    part = part + swap_y(part, 0)
+    part, gram = part[:HALF], part[HALF:]
+    inverse = inverse_of(gram + swap_y(gram, 1))
+    mine, colsq = across_of(part, swap_y(part, 1), inverse)
+
+    colsq = exchange(colsq.reshape(64, 1, RANK), ("core", "x", "z")).reshape(64, RANK)
+    new_momentum, basis, across = momentum_of(core, m, g, left, inverse, mine, swap_core(mine))
     update = update_of(across, colsq, basis)
     return (new_momentum.T, update.T)
 
 
 def solution(mesh):
-    in_specs = (P("row", "col"), P("row", "col"), P("col", None))
-    out_specs = (P("row", "col"), P("row", "col"))
-    return jax.shard_map(body, mesh=mesh, in_specs=in_specs, out_specs=out_specs, check_vma=False)
+    own = jax.sharding.Mesh(mesh.devices.reshape(4, 2, 4, 8), ("y", "core", "x", "z"))
+    whole = P(("y", "core"), ("x", "z"))
+    return jax.shard_map(
+        body, mesh=own, in_specs=(whole, whole, P(("x", "z"), None)), out_specs=(whole, whole), check_vma=False
+    )

time: 97.2 us -> 96.1 us (0.989)
  waiting for transfers between devices: 23.8 us -> 21.5 us
  starting transfers between devices: 24.7 us -> 25.8 us
    ppermute x6 -> x5, waiting for transfers between devices: 9.03 us -> 6.67 us  [the longest x3 5.49 us: swap_y(): return lax.ppermute(block, ('y', 'core'), pairs)]
    ppermute x6 -> x5, starting transfers between devices: 12.1 us -> 12.6 us  [the longest x2 8.11 us: swap_core(): return lax.ppermute(block, 'core', [(0, 1), (1, 0)])]
  transfers between devices with their start and end apart: 8 -> 7, of which waited for: 7 -> 5; matrix products, arithmetic and copies ran while one was open for 0% -> 0% of each run, Pallas kernels for 12% -> 12%
where the time goes in v4:
time: 96.1 us; the launch traced here: 95.8 us
  blocking collectives  26 us (27%)
  starting transfers between devices  25.8 us (27%)
  Pallas kernels  21.7 us (23%)
  waiting for transfers between devices  21.5 us (22%)
    all_to_all x1, blocking collectives, exchange(): return lax.all_to_all(blocks, axes, 0, 0)  26 us
    all_to_all x2, waiting for transfers between devices, exchange(): return lax.all_to_all(blocks, axes, 0, 0)  14.9 us
    all_to_all x2, starting transfers between devices, exchange(): return lax.all_to_all(blocks, axes, 0, 0)  13.3 us
    ppermute x2, starting transfers between devices, swap_core(): return lax.ppermute(block, 'core', [(0, 1), (1, 0)])  8.11 us
    ppermute x3, waiting for transfers between devices, swap_y(): return lax.ppermute(block, ('y', 'core'), pairs)  5.49 us
    pallas_call x1, Pallas kernels, momentum_of(): pl.pallas_call(momentum_kernel, in_specs=[SMEM, ANY, ANY, ANY, WHOLE, WHO...  5.02 us
    ppermute x3, starting transfers between devices, swap_y(): return lax.ppermute(block, ('y', 'core'), pairs)  4.45 us
    pallas_call x1, Pallas kernels, left_of(): pl.pallas_call(left_kernel, in_specs=[ANY, ANY, ANY], out_specs=WHOLE, ou...  4.12 us
  transfers between devices with their start and end apart: 7, of which 5 were waited for; matrix products, arithmetic and copies ran while one was open for 0% of the time, Pallas kernels for 12%

profile of v4, /device:TPU:1, one launch (start us, length us, event | category | flops | bytes accessed | tf_op | source)
XLA Modules:
  0.0 95.8 jit_solution(732672495220469285)
XLA Ops:
  0.6 4.1 %left_part.1 = f32[1024,128]{1,0:T(8,128)S(1)} custom-call(f32[832,1024]{1,0:T(8,128)} %bitcast.13, bf16[832,1024]{1,0:T(8,128)(2,1)} %bitcast.16, f32[832,128]{1,0:T(8,128)} %r_hbm.1), custom_call_target="tpu_custom_call" | custom-call | flops 654311424 | bytes 5111808 | tf_op jit(solution)/shard_map/left_part/pallas_call | solution.py:83
  4.8 26.0 %all_to_all.15.parts_ref = f32[32,32,128]{2,1,0:T(8,128)S(1)} all-to-all(f32[32,32,128]{2,1,0:T(8,128)S(1)} %bitcast.11), channel_id=1, replica_groups=mesh['y'=4,'core'=2,'x'=4,'z'=8] {'x','z'}, dimensions={0} | all-to-all | bytes 1048576 | tf_op jit(solution)/shard_map/all_to_all | solution.py:339
  30.7 0.9 sum_and_spread.1
  31.6 7.6 %all-to-all-start.1 = ((f32[32,32,128]{2,1,0:T(8,128)}), f32[32,32,128]{2,1,0:T(8,128)}, u32[]{:S(2)}, u32[]{:S(2)}) async-start(f32[32,32,128]{2,1,0:T(8,128)} %get-tuple-element.11), calls=%async_computation.1 | async-start | bytes 1048576 | tf_op jit(solution)/shard_map/all_to_all | solution.py:339
  39.2 2.7 %split_blend.1.blend_ref = bf16[1664,1024]{1,0:T(8,128)(2,1)S(1)} custom-call(f32[832,1024]{1,0:T(8,128)} %bitcast.14, bf16[832,1024]{1,0:T(8,128)(2,1)} %bitcast.17, f32[8,128]{1,0:T(8,128)S(1)} %get-tuple-element.12.token_ref), custom_call_target="tpu_custom_call" | custom-call | flops 3407872 | bytes 8519680 | tf_op jit(solution)/shard_map/split_blend/pallas_call | solution.py:132
  41.9 10.9 %all-to-all-done.1 = f32[32,32,128]{2,1,0:T(8,128)} async-done(((f32[32,32,128]{2,1,0:T(8,128)}), f32[32,32,128]{2,1,0:T(8,128)}, u32[]{:S(2)}, u32[]{:S(2)}) %all-to-all-start.1) | async-done | bytes 524320 | tf_op jit(solution)/shard_map/all_to_all | solution.py:339
  52.8 2.4 %weighted_part.1 = (f32[544,128]{1,0:T(8,128)S(1)}, f32[544,128]{1,0:T(8,128)S(1)}) custom-call(s32[1]{0:T(128)} %bitcast.core_ref, f32[1024,128]{1,0:T(8,128)} %bitcast.4.left_ref.left_hbm, bf16[1664,1024]{1,0:T(8,128)(2,1)S(1)} %split_blend.1.blend_ref), custom_call_target="tpu_custom_call" | custom-call | flops 654311424 | bytes 3407872 | tf_op jit(solution)/shard_map/weighted_part/pallas_call | solution.py:169
  55.2 4.6 %collective-permute-start = (f32[544,128]{1,0:T(8,128)S(1)}, f32[544,128]{1,0:T(8,128)S(1)}, u32[]{:S(2)}, u32[]{:S(2)}) collective-permute-start(f32[544,128]{1,0:T(8,128)S(1)} %get-tuple-element.14), channel_id=1, source_target_pairs={{0,32},{32,0},{1,33},{33,1},{2,34},{34,2},{3,35},{35,3},{4,36},{36... | collective-permute-start | bytes 835592 | tf_op jit(solution)/shard_map/ppermute | solution.py:343
  59.9 1.2 %collective-permute-done = f32[544,128]{1,0:T(8,128)S(1)} collective-permute-done((f32[544,128]{1,0:T(8,128)S(1)}, f32[544,128]{1,0:T(8,128)S(1)}, u32[]{:S(2)}, u32[]{:S(2)}) %collective-permute-start) | collective-permute-done | bytes 278560 | tf_op jit(solution)/shard_map/ppermute | solution.py:343
  61.1 2.8 %collective-permute-start.1 = (f32[544,128]{1,0:T(8,128)S(1)}, f32[544,128]{1,0:T(8,128)S(1)}, u32[]{:S(2)}, u32[]{:S(2)}) collective-permute-start(f32[544,128]{1,0:T(8,128)S(1)} %add.9), channel_id=1, source_target_pairs={{0,64},{32,224},{64,0},{96,160},{128,192},{160,96},{192,128},{224,... | collective-permute-start | bytes 835592 | tf_op jit(solution)/shard_map/ppermute | solution.py:348
  63.9 3.9 %collective-permute-done.1 = f32[544,128]{1,0:T(8,128)S(1)} collective-permute-done((f32[544,128]{1,0:T(8,128)S(1)}, f32[544,128]{1,0:T(8,128)S(1)}, u32[]{:S(2)}, u32[]{:S(2)}) %collective-permute-start.1) | collective-permute-done | bytes 278560 | tf_op jit(solution)/shard_map/ppermute | solution.py:348
  67.9 0.4 collective-permute-start.2
  68.3 1.2 %collective-permute-start.3 = (f32[416,128]{1,0:T(8,128)S(1)}, f32[416,128]{1,0:T(8,128)S(1)}, u32[]{:S(2)}, u32[]{:S(2)}) collective-permute-start(f32[416,128]{1,0:T(8,128)S(1)} %slice.9.part_ref), channel_id=1, source_target_pairs={{0,192},{32,96},{64,128},{96,32},{128,64},{160,224},{192,0},{224,1... | collective-permute-start | bytes 638984 | tf_op jit(solution)/shard_map/ppermute | solution.py:348
  69.5 1.5 %collective-permute-done.2 = f32[128,128]{1,0:T(8,128)S(1)} collective-permute-done((f32[128,128]{1,0:T(8,128)S(1)}, f32[128,128]{1,0:T(8,128)S(1)}, u32[]{:S(2)}, u32[]{:S(2)}) %collective-permute-start.2) | collective-permute-done | bytes 65568 | tf_op jit(solution)/shard_map/ppermute | solution.py:348
  71.1 3.8 %inverse_factor.1.inverse_ref = f32[128,128]{1,0:T(8,128)S(1)} custom-call(f32[128,128]{1,0:T(8,128)S(1)} %slice_add_fusion.gram_ref), custom_call_target="tpu_custom_call" | custom-call | flops 64424509440 | bytes 131072 | tf_op jit(solution)/shard_map/inverse_factor/pallas_call | solution.py:221
  74.9 0.0 collective-permute-done.3.got_ref
  74.9 1.0 %across_part.1 = (f32[416,128]{1,0:T(8,128)S(1)}, f32[64,128]{1,0:T(8,128)}) custom-call(f32[416,128]{1,0:T(8,128)S(1)} %slice.9.part_ref, f32[416,128]{1,0:T(8,128)S(1)} %collective-permute-done.3.got_ref, f32[128,128]{1,0:T(8,128)S(1)} %inverse_factor.1.inverse_ref), custom_call_target="tpu_custom_call" | custom-call | flops 81788928 | bytes 851968 | tf_op jit(solution)/shard_map/across_part/pallas_call | solution.py:243
  75.9 3.5 %collective-permute-start.4 = (f32[416,128]{1,0:T(8,128)S(1)}, f32[416,128]{1,0:T(8,128)S(1)}, u32[]{:S(2)}, u32[]{:S(2)}) collective-permute-start(f32[416,128]{1,0:T(8,128)S(1)} %get-tuple-element.15.mine_ref), channel_id=1, source_target_pairs={{0,32},{32,0},{1,33},{33,1},{2,34},{34,2},{3,35},{35,3},{4,36},{36... | collective-permute-start | bytes 638984 | tf_op jit(solution)/shard_map/ppermute | solution.py:343
  79.4 5.6 %all-to-all-start.2 = ((f32[64,1,128]{2,1,0:T(1,128)}), f32[64,1,128]{2,1,0:T(1,128)S(1)}, u32[]{:S(2)}, u32[]{:S(2)}) async-start(f32[64,1,128]{2,1,0:T(1,128)} %bitcast.7), calls=%async_computation.2 | async-start | bytes 65536 | tf_op jit(solution)/shard_map/all_to_all | solution.py:339
  85.0 0.0 collective-permute-done.4.other_ref
  85.0 5.0 %new_momentum.1 = (f32[832,1024]{1,0:T(8,128)}, bf16[384,1024]{1,0:T(8,128)(2,1)S(1)}, f32[832,128]{1,0:T(8,128)S(1)}) custom-call(s32[1]{0:T(128)} %bitcast.core_ref, f32[832,1024]{1,0:T(8,128)} %bitcast.15, bf16[832,1024]{1,0:T(8,128)(2,1)} %bitcast.18, f32[1024,128]{1,0:T(8,128)} %bitcast.4.left_ref.left_hbm, f32[128,128]{1,0:T(8,128)S(1)} %inverse_factor.1.inverse_ref, ...), custom_call_target="tpu_custom_call" | custom-call | flops 436207616 | bytes 8519680 | tf_op jit(solution)/shard_map/new_momentum/pallas_call | solution.py:292
  90.1 3.9 %all-to-all-done.2 = f32[64,1,128]{2,1,0:T(1,128)S(1)} async-done(((f32[64,1,128]{2,1,0:T(1,128)}), f32[64,1,128]{2,1,0:T(1,128)S(1)}, u32[]{:S(2)}, u32[]{:S(2)}) %all-to-all-start.2) | async-done | bytes 32800 | tf_op jit(solution)/shard_map/all_to_all | solution.py:339
  94.0 1.8 %update.1 = bf16[832,1024]{1,0:T(8,128)(2,1)} custom-call(f32[832,128]{1,0:T(8,128)S(1)} %get-tuple-element.17.across_ref, f32[64,128]{1,0:T(8,128)S(1)} %bitcast.12, bf16[384,1024]{1,0:T(8,128)(2,1)S(1)} %get-tuple-element.19.basis_ref), custom_call_target="tpu_custom_call" | custom-call | flops 654311424 | bytes 1703936 | tf_op jit(solution)/shard_map/update/pallas_call | solution.py:326
  (5 shorter events, 0.1 us)
Async XLA Ops:
  31.6 21.2 %all-to-all-start.1 = ((f32[32,32,128]{2,1,0:T(8,128)}), f32[32,32,128]{2,1,0:T(8,128)}, u32[]{:S(2)}, u32[]{:S(2)}) async-start(f32[32,32,128]{2,1,0:T(8,128)} %get-tuple-element.11), calls=%async_computation.1 | async-start | bytes 1048576 | tf_op jit(solution)/shard_map/all_to_all | solution.py:339
  55.2 5.8 %collective-permute-start = (f32[544,128]{1,0:T(8,128)S(1)}, f32[544,128]{1,0:T(8,128)S(1)}, u32[]{:S(2)}, u32[]{:S(2)}) collective-permute-start(f32[544,128]{1,0:T(8,128)S(1)} %get-tuple-element.14), channel_id=1, source_target_pairs={{0,32},{32,0},{1,33},{33,1},{2,34},{34,2},{3,35},{35,3},{4,36},{36... | collective-permute-start | bytes 835592 | tf_op jit(solution)/shard_map/ppermute | solution.py:343
  61.1 6.8 %collective-permute-start.1 = (f32[544,128]{1,0:T(8,128)S(1)}, f32[544,128]{1,0:T(8,128)S(1)}, u32[]{:S(2)}, u32[]{:S(2)}) collective-permute-start(f32[544,128]{1,0:T(8,128)S(1)} %add.9), channel_id=1, source_target_pairs={{0,64},{32,224},{64,0},{96,160},{128,192},{160,96},{192,128},{224,... | collective-permute-start | bytes 835592 | tf_op jit(solution)/shard_map/ppermute | solution.py:348
  67.9 3.2 %collective-permute-start.2 = (f32[128,128]{1,0:T(8,128)S(1)}, f32[128,128]{1,0:T(8,128)S(1)}, u32[]{:S(2)}, u32[]{:S(2)}) collective-permute-start(f32[128,128]{1,0:T(8,128)S(1)} %slice.8), channel_id=1, source_target_pairs={{0,192},{32,96},{64,128},{96,32},{128,64},{160,224},{192,0},{224,1... | collective-permute-start | bytes 196616 | tf_op jit(solution)/shard_map/ppermute | solution.py:348
  68.3 6.6 %collective-permute-start.3 = (f32[416,128]{1,0:T(8,128)S(1)}, f32[416,128]{1,0:T(8,128)S(1)}, u32[]{:S(2)}, u32[]{:S(2)}) collective-permute-start(f32[416,128]{1,0:T(8,128)S(1)} %slice.9.part_ref), channel_id=1, source_target_pairs={{0,192},{32,96},{64,128},{96,32},{128,64},{160,224},{192,0},{224,1... | collective-permute-start | bytes 638984 | tf_op jit(solution)/shard_map/ppermute | solution.py:348
  75.9 9.1 %collective-permute-start.4 = (f32[416,128]{1,0:T(8,128)S(1)}, f32[416,128]{1,0:T(8,128)S(1)}, u32[]{:S(2)}, u32[]{:S(2)}) collective-permute-start(f32[416,128]{1,0:T(8,128)S(1)} %get-tuple-element.15.mine_ref), channel_id=1, source_target_pairs={{0,32},{32,0},{1,33},{33,1},{2,34},{34,2},{3,35},{35,3},{4,36},{36... | collective-permute-start | bytes 638984 | tf_op jit(solution)/shard_map/ppermute | solution.py:343
  79.4 14.6 %all-to-all-start.2 = ((f32[64,1,128]{2,1,0:T(1,128)}), f32[64,1,128]{2,1,0:T(1,128)S(1)}, u32[]{:S(2)}, u32[]{:S(2)}) async-start(f32[64,1,128]{2,1,0:T(1,128)} %bitcast.7), calls=%async_computation.2 | async-start | bytes 65536 | tf_op jit(solution)/shard_map/all_to_all | solution.py:339

commit v5 on v4

--- a/solution.py
+++ b/solution.py
@@ -14,7 +14,7 @@
 
 C = 832
 R = 1024
-DEEP = ((0, 64), (64, 320), (320, 576), (576, 832))
+DEEP = ((0, 320), (320, 832))
 EVEN = tuple((n, n + 208) for n in range(0, C, 208))
 BLOCK = 64
 
@@ -61,7 +61,7 @@
     return copies
 
 
-def left_kernel(m_hbm, g_hbm, r_hbm, left_ref, m_ref, g_ref, r_ref, both_ref, sum_ref, sems, r_sem):
+def left_kernel(core_ref, m_hbm, g_hbm, r_hbm, left_ref, m_ref, g_ref, r_ref, both_ref, sum_ref, sems, r_sem):
     first = pltpu.make_async_copy(r_hbm, r_ref, r_sem)
     first.start()
     loads = start_loads((m_hbm, g_hbm), (m_ref, g_ref), DEEP, sems)
@@ -79,10 +79,10 @@
     left_ref[...] = sum_ref[...].T
 
 
-def left_of(m, g, r):
+def left_of(core, m, g, r):
     return pl.pallas_call(
         left_kernel,
-        in_specs=[ANY, ANY, ANY],
+        in_specs=[SMEM, ANY, ANY, ANY],
         out_specs=WHOLE,
         out_shape=pltpu.VMEM((R, RANK), F32),
         scratch_shapes=[
@@ -97,55 +97,28 @@
         compiler_params=params(14),
         cost_estimate=pl.CostEstimate(flops=6 * R * C * RANK, bytes_accessed=R * C * 6, transcendentals=0),
         name="left_part",
-    )(*far(m, g, r))
-
-
-def spread_kernel(parts_ref, out_ref, token_ref):
-    total = jnp.sum(parts_ref[...], axis=0, keepdims=True)
-    out_ref[...] = jnp.broadcast_to(total, out_ref.shape)
-    token_ref[...] = total[0, :8]
-
-
-def sum_and_spread(parts):
+    )(core, *far(m, g, r))
+
+
+def spread_kernel(parts_ref, out_ref):
+    out_ref[...] = jnp.broadcast_to(jnp.sum(parts_ref[...], axis=0, keepdims=True), out_ref.shape)
+
+
+def sum_and_spread(parts, count):
     return pl.pallas_call(
         spread_kernel,
-        out_shape=[pltpu.VMEM(parts.shape, F32), pltpu.VMEM((8, RANK), F32)],
+        out_shape=pltpu.VMEM((count,) + parts.shape[1:], F32),
         in_specs=[WHOLE],
-        out_specs=[WHOLE, WHOLE],
+        out_specs=WHOLE,
         compiler_params=params(4),
         cost_estimate=pl.CostEstimate(flops=parts.size, bytes_accessed=8 * parts.size, transcendentals=0),
         name="sum_and_spread",
     )(*near(parts))
 
 
-def split_kernel(m_hbm, g_hbm, token_ref, out_ref, m_ref, g_ref, sems):
-    loads = start_loads((m_hbm, g_hbm), (m_ref, g_ref), EVEN, sems)
-    for n, (start, stop) in enumerate(EVEN):
-        for copy in loads[n]:
-            copy.wait()
-        high, low = split(m_ref[start:stop] + g_ref[start:stop].astype(F32))
-        out_ref[start:stop] = high
-        out_ref[C + start : C + stop] = low
-
-
-def split_of(m, g, token):
-    return pl.pallas_call(
-        split_kernel,
-        in_specs=[ANY, ANY, WHOLE],
-        out_specs=WHOLE,
-        out_shape=pltpu.VMEM((2 * C, R), BF16),
-        scratch_shapes=[
-            pltpu.VMEM((C, R), F32),
-            pltpu.VMEM((C, R), BF16),
-            pltpu.SemaphoreType.DMA((len(EVEN), 2)),
-        ],
-        compiler_params=params(8),
-        cost_estimate=pl.CostEstimate(flops=4 * R * C, bytes_accessed=R * C * 10, transcendentals=0),
-        name="split_blend",
-    )(*far(m, g), *near(token))
-
-
-def weighted_kernel(core_ref, left_ref, blend_ref, give_ref, keep_ref, both_ref):
+def weighted_kernel(core_ref, left_ref, m_ref, g_ref, give_ref, keep_ref, both_ref):
+    core = core_ref[0]
+    step = HALF // 2
     left = left_ref[...]
     high, low = split(left)
     rest = (left - high.astype(F32) - low.astype(F32)).astype(BF16)
@@ -156,26 +129,32 @@
     gram = wide[:, :RANK] + (mixed + mixed.T + dot(low, low, ((0,), (0,))))
     give_ref[HALF:] = gram
     keep_ref[HALF:] = gram
-    core = core_ref[0]
-    for out_ref, base in ((give_ref, HALF - core * HALF), (keep_ref, core * HALF)):
-        for step in range(0, HALF, HALF // 2):
-            high = blend_ref[pl.ds(pl.multiple_of(base + step, 16), HALF // 2)]
-            low = blend_ref[pl.ds(pl.multiple_of(base + C + step, 16), HALF // 2)]
-            wide = dot(high, both_ref[...])
-            out_ref[step : step + HALF // 2] = wide[:, :RANK] + wide[:, RANK:] + dot(low, both_ref[:, :RANK])
-
-
-def weighted_of(core, left, blend):
+    theirs, mine = HALF - core * HALF, core * HALF
+    for out_ref, base, start in (
+        (give_ref, theirs, 0),
+        (give_ref, theirs, step),
+        (keep_ref, mine, 0),
+        (keep_ref, mine, step),
+    ):
+        rows = pl.ds(pl.multiple_of(base + start, 16), step)
+        high, low = split(m_ref[rows] + g_ref[rows].astype(F32))
+        wide = dot(high, both_ref[...])
+        out_ref[start : start + step] = wide[:, :RANK] + wide[:, RANK:] + dot(low, both_ref[:, :RANK])
+
+
+def weighted_of(core, left, m, g):
     return pl.pallas_call(
         weighted_kernel,
-        in_specs=[SMEM, WHOLE, WHOLE],
+        in_specs=[SMEM, WHOLE, WHOLE, WHOLE],
         out_specs=[WHOLE, WHOLE],
         out_shape=[pltpu.VMEM((HALF + RANK, RANK), F32)] * 2,
-        scratch_shapes=[pltpu.VMEM((R, 2 * RANK), BF16)],
-        compiler_params=params(6),
-        cost_estimate=pl.CostEstimate(flops=6 * R * C * RANK, bytes_accessed=R * C * 4, transcendentals=0),
+        scratch_shapes=[
+            pltpu.VMEM((R, 2 * RANK), BF16),
+        ],
+        compiler_params=params(8),
+        cost_estimate=pl.CostEstimate(flops=6 * R * C * RANK, bytes_accessed=R * C * 6, transcendentals=0),
         name="weighted_part",
-    )(core, *near(left, blend))
+    )(core, *near(left, m, g))
 
 
 def inverse_kernel(gram_ref, out_ref, work_ref):
@@ -351,12 +330,12 @@
 def body(momentum, gradient, right_factor):
     m, g = momentum.T, gradient.T
     core = lax.axis_index("core").astype(jnp.int32).reshape(1)
-    partial = left_of(m, g, right_factor)
-    spread, token = sum_and_spread(exchange(partial.reshape(32, R // 32, RANK), ("x", "z")))
+    partial = left_of(core, m, g, right_factor)
+    quarter = sum_and_spread(exchange(partial.reshape(4, R // 4, RANK), "x"), 1)
+    spread = sum_and_spread(exchange(quarter.reshape(8, R // 32, RANK), "z"), 32)
     left = exchange(spread, ("x", "z")).reshape(R, RANK)
-    blend = split_of(m, g, token)
-
-    give, part = weighted_of(core, left, blend)
+
+    give, part = weighted_of(core, left, m, g)
     part = part + swap_core(give)
     part = part + swap_y(part, 0)
     part, gram = part[:HALF], part[HALF:]

time: 96.1 us -> 92.8 us (0.966)
  blocking collectives: 26 us -> 44.4 us
  waiting for transfers between devices: 21.5 us -> 11.9 us
  starting transfers between devices: 25.8 us -> 19.7 us
  Pallas kernels: 21.7 us -> 15.7 us
    all_to_all x1 -> x3, blocking collectives: 26 us -> 44.4 us  [exchange(): return lax.all_to_all(blocks, axes, 0, 0)]
    all_to_all x2 -> x1, waiting for transfers between devices: 14.9 us -> 5.26 us  [exchange(): return lax.all_to_all(blocks, axes, 0, 0)]
    all_to_all x2 -> x1, starting transfers between devices: 13.3 us -> 6.13 us  [exchange(): return lax.all_to_all(blocks, axes, 0, 0)]
    pallas_call x4, Pallas kernels: 10 us -> 5.32 us  [the longest x1 3.88 us: left_of(): pl.pallas_call(left_kernel, in_specs=[SMEM, ANY, ANY, ANY], out_specs=WHO...]
    pallas_call x1, Pallas kernels: 5.02 us -> 3.75 us  [momentum_of(): pl.pallas_call(momentum_kernel, in_specs=[SMEM, ANY, ANY, ANY, WHOLE, WHO...]
    ppermute x2, starting transfers between devices: 8.11 us -> 9.09 us  [swap_core(): return lax.ppermute(block, 'core', [(0, 1), (1, 0)])]
  transfers between devices with their start and end apart: 7 -> 6, of which waited for: 5 -> 4; matrix products, arithmetic and copies ran while one was open for 0% -> 0% of each run, Pallas kernels for 12% -> 8%
where the time goes in v5:
time: 92.8 us; the launch traced here: 92.6 us
  blocking collectives  44.4 us (48%)
  starting transfers between devices  19.7 us (21%)
  Pallas kernels  15.7 us (17%)
  waiting for transfers between devices  11.9 us (13%)
    all_to_all x3, blocking collectives, exchange(): return lax.all_to_all(blocks, axes, 0, 0)  44.4 us
    ppermute x2, starting transfers between devices, swap_core(): return lax.ppermute(block, 'core', [(0, 1), (1, 0)])  9.09 us
    all_to_all x1, starting transfers between devices, exchange(): return lax.all_to_all(blocks, axes, 0, 0)  6.13 us
    ppermute x3, waiting for transfers between devices, swap_y(): return lax.ppermute(block, ('y', 'core'), pairs)  5.49 us
    all_to_all x1, waiting for transfers between devices, exchange(): return lax.all_to_all(blocks, axes, 0, 0)  5.26 us
    ppermute x3, starting transfers between devices, swap_y(): return lax.ppermute(block, ('y', 'core'), pairs)  4.46 us
    pallas_call x1, Pallas kernels, left_of(): pl.pallas_call(left_kernel, in_specs=[SMEM, ANY, ANY, ANY], out_specs=WHO...  3.88 us
    pallas_call x1, Pallas kernels, inverse_of(): pl.pallas_call(inverse_kernel, out_shape=pltpu.VMEM((RANK, RANK), F32), i...  3.8 us
  transfers between devices with their start and end apart: 6, of which 4 were waited for; matrix products, arithmetic and copies ran while one was open for 0% of the time, Pallas kernels for 8%

profile of v5, /device:TPU:1, one launch (start us, length us, event | category | flops | bytes accessed | tf_op | source)
XLA Modules:
  0.0 92.6 jit_solution(6754641216016935564)
XLA Ops:
  0.6 0.0 copy-start
  0.6 0.0 copy-start.1
  0.7 3.9 %left_part.1 = f32[1024,128]{1,0:T(8,128)S(1)} custom-call(s32[1]{0:T(128)} %bitcast.core_ref, f32[832,1024]{1,0:T(8,128)} %bitcast.12, bf16[832,1024]{1,0:T(8,128)(2,1)} %bitcast.15, f32[832,128]{1,0:T(8,128)} %r_hbm.1), custom_call_target="tpu_custom_call" | custom-call | flops 654311424 | bytes 5111808 | tf_op jit(solution)/shard_map/left_part/pallas_call | solution.py:83
  4.5 13.2 %all_to_all.20.parts_ref = f32[4,256,128]{2,1,0:T(8,128)S(1)} all-to-all(f32[4,256,128]{2,1,0:T(8,128)S(1)} %bitcast.20), channel_id=1, replica_groups=mesh['y'=4,'core'=2,'x'=4,'z'=8] {'x'}, dimensions={0} | all-to-all | bytes 1048576 | tf_op jit(solution)/shard_map/all_to_all | solution.py:318
  17.7 16.1 %all_to_all.21.parts_ref = f32[8,32,128]{2,1,0:T(8,128)S(1)} all-to-all(f32[8,32,128]{2,1,0:T(8,128)S(1)} %bitcast.21), channel_id=1, replica_groups=mesh['y'=4,'core'=2,'x'=4,'z'=8] {'z'}, dimensions={0} | all-to-all | bytes 262144 | tf_op jit(solution)/shard_map/all_to_all | solution.py:318
  33.8 0.1 sum_and_spread.3
  33.9 15.1 %all_to_all.22 = f32[32,32,128]{2,1,0:T(8,128)S(1)} all-to-all(f32[32,32,128]{2,1,0:T(8,128)S(1)} %sum_and_spread.3), channel_id=1, replica_groups=mesh['y'=4,'core'=2,'x'=4,'z'=8] {'x','z'}, dimensions={0} | all-to-all | bytes 1048576 | tf_op jit(solution)/shard_map/all_to_all | solution.py:318
  49.0 1.4 %weighted_part.1 = (f32[544,128]{1,0:T(8,128)S(1)}, f32[544,128]{1,0:T(8,128)S(1)}) custom-call(s32[1]{0:T(128)} %bitcast.core_ref, f32[1024,128]{1,0:T(8,128)S(1)} %bitcast.18, f32[832,1024]{1,0:T(8,128)S(1)} %bitcast.14, bf16[832,1024]{1,0:T(8,128)(2,1)S(1)} %bitcast.17), custom_call_target="tpu_custom_call" | custom-call | flops 654311424 | bytes 5111808 | tf_op jit(solution)/shard_map/weighted_part/pallas_call | solution.py:146
  50.4 5.6 %collective-permute-start = (f32[544,128]{1,0:T(8,128)S(1)}, f32[544,128]{1,0:T(8,128)S(1)}, u32[]{:S(2)}, u32[]{:S(2)}) collective-permute-start(f32[544,128]{1,0:T(8,128)S(1)} %get-tuple-element.10), channel_id=1, source_target_pairs={{0,32},{32,0},{1,33},{33,1},{2,34},{34,2},{3,35},{35,3},{4,36},{36... | collective-permute-start | bytes 835592 | tf_op jit(solution)/shard_map/ppermute | solution.py:322
  56.0 1.2 %collective-permute-done = f32[544,128]{1,0:T(8,128)S(1)} collective-permute-done((f32[544,128]{1,0:T(8,128)S(1)}, f32[544,128]{1,0:T(8,128)S(1)}, u32[]{:S(2)}, u32[]{:S(2)}) %collective-permute-start) | collective-permute-done | bytes 278560 | tf_op jit(solution)/shard_map/ppermute | solution.py:322
  57.2 2.8 %collective-permute-start.1 = (f32[544,128]{1,0:T(8,128)S(1)}, f32[544,128]{1,0:T(8,128)S(1)}, u32[]{:S(2)}, u32[]{:S(2)}) collective-permute-start(f32[544,128]{1,0:T(8,128)S(1)} %add.9), channel_id=1, source_target_pairs={{0,64},{32,224},{64,0},{96,160},{128,192},{160,96},{192,128},{224,... | collective-permute-start | bytes 835592 | tf_op jit(solution)/shard_map/ppermute | solution.py:327
  60.0 3.9 %collective-permute-done.1 = f32[544,128]{1,0:T(8,128)S(1)} collective-permute-done((f32[544,128]{1,0:T(8,128)S(1)}, f32[544,128]{1,0:T(8,128)S(1)}, u32[]{:S(2)}, u32[]{:S(2)}) %collective-permute-start.1) | collective-permute-done | bytes 278560 | tf_op jit(solution)/shard_map/ppermute | solution.py:327
  64.0 0.4 collective-permute-start.2
  64.5 1.2 %collective-permute-start.3 = (f32[416,128]{1,0:T(8,128)S(1)}, f32[416,128]{1,0:T(8,128)S(1)}, u32[]{:S(2)}, u32[]{:S(2)}) collective-permute-start(f32[416,128]{1,0:T(8,128)S(1)} %slice.9.part_ref), channel_id=1, source_target_pairs={{0,192},{32,96},{64,128},{96,32},{128,64},{160,224},{192,0},{224,1... | collective-permute-start | bytes 638984 | tf_op jit(solution)/shard_map/ppermute | solution.py:327
  65.7 1.5 %collective-permute-done.2 = f32[128,128]{1,0:T(8,128)S(1)} collective-permute-done((f32[128,128]{1,0:T(8,128)S(1)}, f32[128,128]{1,0:T(8,128)S(1)}, u32[]{:S(2)}, u32[]{:S(2)}) %collective-permute-start.2) | collective-permute-done | bytes 65568 | tf_op jit(solution)/shard_map/ppermute | solution.py:327
  67.3 0.0 copy-start.3
  67.3 3.8 %inverse_factor.1.inverse_ref = f32[128,128]{1,0:T(8,128)S(1)} custom-call(f32[128,128]{1,0:T(8,128)S(1)} %slice_add_fusion.gram_ref), custom_call_target="tpu_custom_call" | custom-call | flops 64424509440 | bytes 131072 | tf_op jit(solution)/shard_map/inverse_factor/pallas_call | solution.py:200
  71.1 0.0 collective-permute-done.3.got_ref
  71.1 1.0 %across_part.1 = (f32[416,128]{1,0:T(8,128)S(1)}, f32[64,128]{1,0:T(8,128)}) custom-call(f32[416,128]{1,0:T(8,128)S(1)} %slice.9.part_ref, f32[416,128]{1,0:T(8,128)S(1)} %collective-permute-done.3.got_ref, f32[128,128]{1,0:T(8,128)S(1)} %inverse_factor.1.inverse_ref), custom_call_target="tpu_custom_call" | custom-call | flops 81788928 | bytes 851968 | tf_op jit(solution)/shard_map/across_part/pallas_call | solution.py:222
  72.1 3.4 %collective-permute-start.4 = (f32[416,128]{1,0:T(8,128)S(1)}, f32[416,128]{1,0:T(8,128)S(1)}, u32[]{:S(2)}, u32[]{:S(2)}) collective-permute-start(f32[416,128]{1,0:T(8,128)S(1)} %get-tuple-element.11.mine_ref), channel_id=1, source_target_pairs={{0,32},{32,0},{1,33},{33,1},{2,34},{34,2},{3,35},{35,3},{4,36},{36... | collective-permute-start | bytes 638984 | tf_op jit(solution)/shard_map/ppermute | solution.py:322
  75.5 6.1 %all-to-all-start.3 = ((f32[64,1,128]{2,1,0:T(1,128)}), f32[64,1,128]{2,1,0:T(1,128)S(1)}, u32[]{:S(2)}, u32[]{:S(2)}) async-start(f32[64,1,128]{2,1,0:T(1,128)} %bitcast.8), calls=%async_computation.3 | async-start | bytes 65536 | tf_op jit(solution)/shard_map/all_to_all | solution.py:318
  81.7 3.7 %new_momentum.1 = (f32[832,1024]{1,0:T(8,128)}, bf16[384,1024]{1,0:T(8,128)(2,1)S(1)}, f32[832,128]{1,0:T(8,128)S(1)}) custom-call(s32[1]{0:T(128)} %bitcast.core_ref, f32[832,1024]{1,0:T(8,128)} %bitcast.13, bf16[832,1024]{1,0:T(8,128)(2,1)} %bitcast.16, f32[1024,128]{1,0:T(8,128)S(1)} %bitcast.19, f32[128,128]{1,0:T(8,128)S(1)} %inverse_factor.1.inverse_ref, ...), custom_call_target="tpu_custom_call" | custom-call | flops 436207616 | bytes 8519680 | tf_op jit(solution)/shard_map/new_momentum/pallas_call | solution.py:271
  85.4 5.3 %all-to-all-done.3 = f32[64,1,128]{2,1,0:T(1,128)S(1)} async-done(((f32[64,1,128]{2,1,0:T(1,128)}), f32[64,1,128]{2,1,0:T(1,128)S(1)}, u32[]{:S(2)}, u32[]{:S(2)}) %all-to-all-start.3) | async-done | bytes 32800 | tf_op jit(solution)/shard_map/all_to_all | solution.py:318
  90.7 1.8 %update.1 = bf16[832,1024]{1,0:T(8,128)(2,1)} custom-call(f32[832,128]{1,0:T(8,128)S(1)} %get-tuple-element.13.across_ref, f32[64,128]{1,0:T(8,128)S(1)} %bitcast.22, bf16[384,1024]{1,0:T(8,128)(2,1)S(1)} %get-tuple-element.15.basis_ref), custom_call_target="tpu_custom_call" | custom-call | flops 654311424 | bytes 1703936 | tf_op jit(solution)/shard_map/update/pallas_call | solution.py:305
  (12 shorter events, 0.1 us)
Async XLA Ops:
  0.6 48.4 %copy-start = (f32[1024,832]{0,1:T(8,128)S(1)}, f32[1024,832]{0,1:T(8,128)}, u32[]{:S(2)}) copy-start(f32[1024,832]{0,1:T(8,128)} %param.3) | copy-start | bytes 10223620
  0.6 48.4 %copy-start.1 = (bf16[1024,832]{0,1:T(8,128)(2,1)S(1)}, bf16[1024,832]{0,1:T(8,128)(2,1)}, u32[]{:S(2)}) copy-start(bf16[1024,832]{0,1:T(8,128)(2,1)} %param.4) | copy-start | bytes 5111812
  49.0 15.0 %copy-start.2 = (f32[32,32,128]{2,1,0:T(8,128)}, f32[32,32,128]{2,1,0:T(8,128)S(1)}, u32[]{:S(2)}) copy-start(f32[32,32,128]{2,1,0:T(8,128)S(1)} %all_to_all.22) | copy-start | bytes 1572868
  50.4 6.8 %collective-permute-start = (f32[544,128]{1,0:T(8,128)S(1)}, f32[544,128]{1,0:T(8,128)S(1)}, u32[]{:S(2)}, u32[]{:S(2)}) collective-permute-start(f32[544,128]{1,0:T(8,128)S(1)} %get-tuple-element.10), channel_id=1, source_target_pairs={{0,32},{32,0},{1,33},{33,1},{2,34},{34,2},{3,35},{35,3},{4,36},{36... | collective-permute-start | bytes 835592 | tf_op jit(solution)/shard_map/ppermute | solution.py:322
  57.2 6.8 %collective-permute-start.1 = (f32[544,128]{1,0:T(8,128)S(1)}, f32[544,128]{1,0:T(8,128)S(1)}, u32[]{:S(2)}, u32[]{:S(2)}) collective-permute-start(f32[544,128]{1,0:T(8,128)S(1)} %add.9), channel_id=1, source_target_pairs={{0,64},{32,224},{64,0},{96,160},{128,192},{160,96},{192,128},{224,... | collective-permute-start | bytes 835592 | tf_op jit(solution)/shard_map/ppermute | solution.py:327
  64.0 3.2 %collective-permute-start.2 = (f32[128,128]{1,0:T(8,128)S(1)}, f32[128,128]{1,0:T(8,128)S(1)}, u32[]{:S(2)}, u32[]{:S(2)}) collective-permute-start(f32[128,128]{1,0:T(8,128)S(1)} %slice.8), channel_id=1, source_target_pairs={{0,192},{32,96},{64,128},{96,32},{128,64},{160,224},{192,0},{224,1... | collective-permute-start | bytes 196616 | tf_op jit(solution)/shard_map/ppermute | solution.py:327
  64.5 6.6 %collective-permute-start.3 = (f32[416,128]{1,0:T(8,128)S(1)}, f32[416,128]{1,0:T(8,128)S(1)}, u32[]{:S(2)}, u32[]{:S(2)}) collective-permute-start(f32[416,128]{1,0:T(8,128)S(1)} %slice.9.part_ref), channel_id=1, source_target_pairs={{0,192},{32,96},{64,128},{96,32},{128,64},{160,224},{192,0},{224,1... | collective-permute-start | bytes 638984 | tf_op jit(solution)/shard_map/ppermute | solution.py:327
  67.3 14.4 %copy-start.3 = (f32[32,32,128]{2,1,0:T(8,128)S(1)}, f32[32,32,128]{2,1,0:T(8,128)}, u32[]{:S(2)}) copy-start(f32[32,32,128]{2,1,0:T(8,128)} %copy-done.2) | copy-start | bytes 1572868
  72.1 9.6 %collective-permute-start.4 = (f32[416,128]{1,0:T(8,128)S(1)}, f32[416,128]{1,0:T(8,128)S(1)}, u32[]{:S(2)}, u32[]{:S(2)}) collective-permute-start(f32[416,128]{1,0:T(8,128)S(1)} %get-tuple-element.11.mine_ref), channel_id=1, source_target_pairs={{0,32},{32,0},{1,33},{33,1},{2,34},{34,2},{3,35},{35,3},{4,36},{36... | collective-permute-start | bytes 638984 | tf_op jit(solution)/shard_map/ppermute | solution.py:322
  75.5 15.2 %all-to-all-start.3 = ((f32[64,1,128]{2,1,0:T(1,128)}), f32[64,1,128]{2,1,0:T(1,128)S(1)}, u32[]{:S(2)}, u32[]{:S(2)}) async-start(f32[64,1,128]{2,1,0:T(1,128)} %bitcast.8), calls=%async_computation.3 | async-start | bytes 65536 | tf_op jit(solution)/shard_map/all_to_all | solution.py:318

commit v6 on v5

--- a/solution.py
+++ b/solution.py
@@ -116,9 +116,16 @@
     )(*near(parts))
 
 
-def weighted_kernel(core_ref, left_ref, m_ref, g_ref, give_ref, keep_ref, both_ref):
-    core = core_ref[0]
-    step = HALF // 2
+def product(core_ref, away, both_ref, m_ref, g_ref, out_ref):
+    base = (1 - core_ref[0] if away else core_ref[0]) * HALF
+    for start in range(0, HALF, HALF // 2):
+        rows = pl.ds(pl.multiple_of(base + start, 16), HALF // 2)
+        high, low = split(m_ref[rows] + g_ref[rows].astype(F32))
+        wide = dot(high, both_ref[...])
+        out_ref[start : start + HALF // 2] = wide[:, :RANK] + wide[:, RANK:] + dot(low, both_ref[:, :RANK])
+
+
+def give_kernel(core_ref, left_ref, m_ref, g_ref, give_ref, both_ref):
     left = left_ref[...]
     high, low = split(left)
     rest = (left - high.astype(F32) - low.astype(F32)).astype(BF16)
@@ -126,42 +133,44 @@
     both_ref[:, RANK:] = low
     wide = dot(high, both_ref[...], ((0,), (0,)))
     mixed = wide[:, RANK:] + dot(high, rest, ((0,), (0,)))
-    gram = wide[:, :RANK] + (mixed + mixed.T + dot(low, low, ((0,), (0,))))
-    give_ref[HALF:] = gram
-    keep_ref[HALF:] = gram
-    theirs, mine = HALF - core * HALF, core * HALF
-    for out_ref, base, start in (
-        (give_ref, theirs, 0),
-        (give_ref, theirs, step),
-        (keep_ref, mine, 0),
-        (keep_ref, mine, step),
-    ):
-        rows = pl.ds(pl.multiple_of(base + start, 16), step)
-        high, low = split(m_ref[rows] + g_ref[rows].astype(F32))
-        wide = dot(high, both_ref[...])
-        out_ref[start : start + step] = wide[:, :RANK] + wide[:, RANK:] + dot(low, both_ref[:, :RANK])
+    give_ref[HALF:] = wide[:, :RANK] + (mixed + mixed.T + dot(low, low, ((0,), (0,))))
+    product(core_ref, True, both_ref, m_ref, g_ref, give_ref)
+
+
+def keep_kernel(core_ref, both_ref, m_ref, g_ref, give_ref, keep_ref):
+    product(core_ref, False, both_ref, m_ref, g_ref, keep_ref)
+    keep_ref[HALF:] = give_ref[HALF:]
 
 
 def weighted_of(core, left, m, g):
-    return pl.pallas_call(
-        weighted_kernel,
+    out = pltpu.VMEM((HALF + RANK, RANK), F32)
+    cost = pl.CostEstimate(flops=3 * R * C * RANK, bytes_accessed=R * C * 3, transcendentals=0)
+    give, both = pl.pallas_call(
+        give_kernel,
         in_specs=[SMEM, WHOLE, WHOLE, WHOLE],
         out_specs=[WHOLE, WHOLE],
-        out_shape=[pltpu.VMEM((HALF + RANK, RANK), F32)] * 2,
-        scratch_shapes=[
-            pltpu.VMEM((R, 2 * RANK), BF16),
-        ],
+        out_shape=[out, pltpu.VMEM((R, 2 * RANK), BF16)],
         compiler_params=params(8),
-        cost_estimate=pl.CostEstimate(flops=6 * R * C * RANK, bytes_accessed=R * C * 6, transcendentals=0),
-        name="weighted_part",
+        cost_estimate=cost,
+        name="weighted_give",
     )(core, *near(left, m, g))
-
-
-def inverse_kernel(gram_ref, out_ref, work_ref):
+    keep = pl.pallas_call(
+        keep_kernel,
+        in_specs=[SMEM, WHOLE, WHOLE, WHOLE, WHOLE],
+        out_specs=WHOLE,
+        out_shape=out,
+        compiler_params=params(8),
+        cost_estimate=cost,
+        name="weighted_keep",
+    )(core, *near(both, m, g, give))
+    return give, keep
+
+
+def inverse_kernel(gram_ref, got_ref, out_ref, work_ref):
     n, b, t = RANK, BLOCK, 8
     row = lax.broadcasted_iota(jnp.int32, (n, n), 0)
     column = lax.broadcasted_iota(jnp.int32, (n, n), 1)
-    work_ref[:, :n] = gram_ref[...]
+    work_ref[:, :n] = gram_ref[...] + got_ref[...]
     work_ref[:, n:] = jnp.where(row == column, 1.0, 0.0)
     place = lax.broadcasted_iota(jnp.int32, (t, n), 0)
     for o in range(0, n, b):
@@ -196,17 +205,17 @@
             work_ref[o + b :] -= dot(upper_block[:, o + b :], done, ((0,), (0,)), HIGH)
 
 
-def inverse_of(gram):
+def inverse_of(gram, got):
     return pl.pallas_call(
         inverse_kernel,
         out_shape=pltpu.VMEM((RANK, RANK), F32),
-        in_specs=[WHOLE],
+        in_specs=[WHOLE, WHOLE],
         out_specs=WHOLE,
         scratch_shapes=[pltpu.VMEM((RANK, 2 * RANK), F32)],
         compiler_params=params(2),
         cost_estimate=pl.CostEstimate(flops=60 << 30, bytes_accessed=1 << 17, transcendentals=0),
         name="inverse_factor",
-    )(*near(gram))
+    )(*near(gram, got))
 
 
 def across_kernel(part_ref, got_ref, inverse_ref, across_ref, colsq_ref):
@@ -337,9 +346,10 @@
 
     give, part = weighted_of(core, left, m, g)
     part = part + swap_core(give)
+    part, gram = part[:HALF], part[HALF:]
+    gram = gram + swap_y(gram, 0)
+    inverse = inverse_of(gram, swap_y(gram, 1))
     part = part + swap_y(part, 0)
-    part, gram = part[:HALF], part[HALF:]
-    inverse = inverse_of(gram + swap_y(gram, 1))
     mine, colsq = across_of(part, swap_y(part, 1), inverse)
 
     colsq = exchange(colsq.reshape(64, 1, RANK), ("core", "x", "z")).reshape(64, RANK)

time: 92.8 us -> 90.5 us (0.975)
  starting transfers between devices: 19.7 us -> 16.4 us
    ppermute x2, starting transfers between devices: 9.09 us -> 7.11 us  [swap_core(): return lax.ppermute(block, 'core', [(0, 1), (1, 0)])]
    ppermute x3 -> x4, waiting for transfers between devices: 5.49 us -> 6.91 us  [swap_y(): return lax.ppermute(block, ('y', 'core'), pairs)]
    ppermute x3 -> x4, starting transfers between devices: 4.46 us -> 3.13 us  [swap_y(): return lax.ppermute(block, ('y', 'core'), pairs)]
  transfers between devices with their start and end apart: 6 -> 7, of which waited for: 4 -> 5; matrix products, arithmetic and copies ran while one was open for 0% -> 0% of each run, Pallas kernels for 8% -> 9%
where the time goes in v6:
time: 90.5 us; the launch traced here: 90.2 us
  blocking collectives  44.4 us (49%)
  starting transfers between devices  16.4 us (18%)
  Pallas kernels  15.9 us (18%)
  waiting for transfers between devices  12.7 us (14%)
    all_to_all x3, blocking collectives, exchange(): return lax.all_to_all(blocks, axes, 0, 0)  44.4 us
    ppermute x2, starting transfers between devices, swap_core(): return lax.ppermute(block, 'core', [(0, 1), (1, 0)])  7.11 us
    ppermute x4, waiting for transfers between devices, swap_y(): return lax.ppermute(block, ('y', 'core'), pairs)  6.91 us
    all_to_all x1, starting transfers between devices, exchange(): return lax.all_to_all(blocks, axes, 0, 0)  6.11 us
    all_to_all x1, waiting for transfers between devices, exchange(): return lax.all_to_all(blocks, axes, 0, 0)  5.28 us
    pallas_call x1, Pallas kernels, left_of(): pl.pallas_call(left_kernel, in_specs=[SMEM, ANY, ANY, ANY], out_specs=WHO...  3.88 us
    pallas_call x1, Pallas kernels, inverse_of(): pl.pallas_call(inverse_kernel, out_shape=pltpu.VMEM((RANK, RANK), F32), i...  3.8 us
    pallas_call x1, Pallas kernels, momentum_of(): pl.pallas_call(momentum_kernel, in_specs=[SMEM, ANY, ANY, ANY, WHOLE, WHO...  3.75 us
  transfers between devices with their start and end apart: 7, of which 5 were waited for; matrix products, arithmetic and copies ran while one was open for 0% of the time, Pallas kernels for 9%

profile of v6, /device:TPU:1, one launch (start us, length us, event | category | flops | bytes accessed | tf_op | source)
XLA Modules:
  0.0 90.2 jit_solution(16524432064530914566)
XLA Ops:
  0.6 0.0 copy-start
  0.7 3.9 %left_part.1 = f32[1024,128]{1,0:T(8,128)S(1)} custom-call(s32[1]{0:T(128)} %bitcast.core_ref, f32[832,1024]{1,0:T(8,128)} %bitcast.12, bf16[832,1024]{1,0:T(8,128)(2,1)} %bitcast.16, f32[832,128]{1,0:T(8,128)} %r_hbm.1), custom_call_target="tpu_custom_call" | custom-call | flops 654311424 | bytes 5111808 | tf_op jit(solution)/shard_map/left_part/pallas_call | solution.py:83
  4.5 13.2 %all_to_all.20.parts_ref = f32[4,256,128]{2,1,0:T(8,128)S(1)} all-to-all(f32[4,256,128]{2,1,0:T(8,128)S(1)} %bitcast.22), channel_id=1, replica_groups=mesh['y'=4,'core'=2,'x'=4,'z'=8] {'x'}, dimensions={0} | all-to-all | bytes 1048576 | tf_op jit(solution)/shard_map/all_to_all | solution.py:327
  17.7 16.1 %all_to_all.21.parts_ref = f32[8,32,128]{2,1,0:T(8,128)S(1)} all-to-all(f32[8,32,128]{2,1,0:T(8,128)S(1)} %bitcast.23), channel_id=1, replica_groups=mesh['y'=4,'core'=2,'x'=4,'z'=8] {'z'}, dimensions={0} | all-to-all | bytes 262144 | tf_op jit(solution)/shard_map/all_to_all | solution.py:327
  33.8 0.1 sum_and_spread.3
  33.9 15.1 %all_to_all.22 = f32[32,32,128]{2,1,0:T(8,128)S(1)} all-to-all(f32[32,32,128]{2,1,0:T(8,128)S(1)} %sum_and_spread.3), channel_id=1, replica_groups=mesh['y'=4,'core'=2,'x'=4,'z'=8] {'x','z'}, dimensions={0} | all-to-all | bytes 1048576 | tf_op jit(solution)/shard_map/all_to_all | solution.py:327
  49.0 0.9 %weighted_give.1 = (f32[544,128]{1,0:T(8,128)S(1)}, bf16[1024,256]{1,0:T(8,128)(2,1)S(1)}) custom-call(s32[1]{0:T(128)} %bitcast.core_ref, f32[1024,128]{1,0:T(8,128)S(1)} %bitcast.20, f32[832,1024]{1,0:T(8,128)S(1)} %bitcast.14, bf16[832,1024]{1,0:T(8,128)(2,1)S(1)} %bitcast.18), custom_call_target="tpu_custom_call" | custom-call | flops 327155712 | bytes 2555904 | tf_op jit(solution)/shard_map/weighted_give/pallas_call | solution.py:148
  49.9 5.6 %collective-permute-start = (f32[544,128]{1,0:T(8,128)S(1)}, f32[544,128]{1,0:T(8,128)S(1)}, u32[]{:S(2)}, u32[]{:S(2)}) collective-permute-start(f32[544,128]{1,0:T(8,128)S(1)} %get-tuple-element.10.give_ref), channel_id=1, source_target_pairs={{0,32},{32,0},{1,33},{33,1},{2,34},{34,2},{3,35},{35,3},{4,36},{36... | collective-permute-start | bytes 835592 | tf_op jit(solution)/shard_map/ppermute | solution.py:331
  55.6 0.6 weighted_keep.1
  56.2 0.5 collective-permute-done
  56.8 2.8 %collective-permute-start.1 = (f32[128,128]{1,0:T(8,128)S(1)}, f32[128,128]{1,0:T(8,128)S(1)}, u32[]{:S(2)}, u32[]{:S(2)}) collective-permute-start(f32[128,128]{1,0:T(8,128)S(1)} %slice.8), channel_id=1, source_target_pairs={{0,64},{32,224},{64,0},{96,160},{128,192},{160,96},{192,128},{224,... | collective-permute-start | bytes 196616 | tf_op jit(solution)/shard_map/ppermute | solution.py:336
  59.6 0.1 collective-permute-start.3
  59.7 1.5 %collective-permute-done.1 = f32[128,128]{1,0:T(8,128)S(1)} collective-permute-done((f32[128,128]{1,0:T(8,128)S(1)}, f32[128,128]{1,0:T(8,128)S(1)}, u32[]{:S(2)}, u32[]{:S(2)}) %collective-permute-start.1) | collective-permute-done | bytes 65568 | tf_op jit(solution)/shard_map/ppermute | solution.py:336
  61.3 0.1 collective-permute-start.2
  61.4 4.2 %collective-permute-done.3 = f32[416,128]{1,0:T(8,128)S(1)} collective-permute-done((f32[416,128]{1,0:T(8,128)S(1)}, f32[416,128]{1,0:T(8,128)S(1)}, u32[]{:S(2)}, u32[]{:S(2)}) %collective-permute-start.3) | collective-permute-done | bytes 213024 | tf_op jit(solution)/shard_map/ppermute | solution.py:336
  65.7 0.1 collective-permute-start.4
  65.8 3.8 %inverse_factor.1.inverse_ref = f32[128,128]{1,0:T(8,128)S(1)} custom-call(f32[128,128]{1,0:T(8,128)S(1)} %slice_add_fusion.gram_ref, f32[128,128]{1,0:T(8,128)S(1)} %collective-permute-done.2.got_ref), custom_call_target="tpu_custom_call" | custom-call | flops 64424509440 | bytes 131072 | tf_op jit(solution)/shard_map/inverse_factor/pallas_call | solution.py:209
  69.6 1.2 %collective-permute-done.4.got_ref = f32[416,128]{1,0:T(8,128)S(1)} collective-permute-done((f32[416,128]{1,0:T(8,128)S(1)}, f32[416,128]{1,0:T(8,128)S(1)}, u32[]{:S(2)}, u32[]{:S(2)}) %collective-permute-start.4) | collective-permute-done | bytes 213024 | tf_op jit(solution)/shard_map/ppermute | solution.py:336
  70.7 1.0 %across_part.1 = (f32[416,128]{1,0:T(8,128)S(1)}, f32[64,128]{1,0:T(8,128)}) custom-call(f32[416,128]{1,0:T(8,128)S(1)} %slice_add_fusion.1.part_ref, f32[416,128]{1,0:T(8,128)S(1)} %collective-permute-done.4.got_ref, f32[128,128]{1,0:T(8,128)S(1)} %inverse_factor.1.inverse_ref), custom_call_target="tpu_custom_call" | custom-call | flops 81788928 | bytes 851968 | tf_op jit(solution)/shard_map/across_part/pallas_call | solution.py:231
  71.7 1.5 %collective-permute-start.5 = (f32[416,128]{1,0:T(8,128)S(1)}, f32[416,128]{1,0:T(8,128)S(1)}, u32[]{:S(2)}, u32[]{:S(2)}) collective-permute-start(f32[416,128]{1,0:T(8,128)S(1)} %get-tuple-element.11.mine_ref), channel_id=1, source_target_pairs={{0,32},{32,0},{1,33},{33,1},{2,34},{34,2},{3,35},{35,3},{4,36},{36... | collective-permute-start | bytes 638984 | tf_op jit(solution)/shard_map/ppermute | solution.py:331
  73.2 6.1 %all-to-all-start.3 = ((f32[64,1,128]{2,1,0:T(1,128)}), f32[64,1,128]{2,1,0:T(1,128)S(1)}, u32[]{:S(2)}, u32[]{:S(2)}) async-start(f32[64,1,128]{2,1,0:T(1,128)} %bitcast.8), calls=%async_computation.3 | async-start | bytes 65536 | tf_op jit(solution)/shard_map/all_to_all | solution.py:327
  79.3 3.7 %new_momentum.1 = (f32[832,1024]{1,0:T(8,128)}, bf16[384,1024]{1,0:T(8,128)(2,1)S(1)}, f32[832,128]{1,0:T(8,128)S(1)}) custom-call(s32[1]{0:T(128)} %bitcast.core_ref, f32[832,1024]{1,0:T(8,128)} %bitcast.13, bf16[832,1024]{1,0:T(8,128)(2,1)} %bitcast.17, f32[1024,128]{1,0:T(8,128)S(1)} %bitcast.21, f32[128,128]{1,0:T(8,128)S(1)} %inverse_factor.1.inverse_ref, ...), custom_call_target="tpu_custom_call" | custom-call | flops 436207616 | bytes 8519680 | tf_op jit(solution)/shard_map/new_momentum/pallas_call | solution.py:280
  83.1 5.3 %all-to-all-done.3 = f32[64,1,128]{2,1,0:T(1,128)S(1)} async-done(((f32[64,1,128]{2,1,0:T(1,128)}), f32[64,1,128]{2,1,0:T(1,128)S(1)}, u32[]{:S(2)}, u32[]{:S(2)}) %all-to-all-start.3) | async-done | bytes 32800 | tf_op jit(solution)/shard_map/all_to_all | solution.py:327
  88.4 1.9 %update.1 = bf16[832,1024]{1,0:T(8,128)(2,1)} custom-call(f32[832,128]{1,0:T(8,128)S(1)} %get-tuple-element.13.across_ref, f32[64,128]{1,0:T(8,128)S(1)} %bitcast.24, bf16[384,1024]{1,0:T(8,128)(2,1)S(1)} %get-tuple-element.15.basis_ref), custom_call_target="tpu_custom_call" | custom-call | flops 654311424 | bytes 1703936 | tf_op jit(solution)/shard_map/update/pallas_call | solution.py:314
  (15 shorter events, 0.1 us)
Async XLA Ops:
  0.6 48.4 %copy-start = (f32[1024,832]{0,1:T(8,128)S(1)}, f32[1024,832]{0,1:T(8,128)}, u32[]{:S(2)}) copy-start(f32[1024,832]{0,1:T(8,128)} %param.3) | copy-start | bytes 10223620
  0.6 48.4 %copy-start.1 = (bf16[1024,832]{0,1:T(8,128)(2,1)S(1)}, bf16[1024,832]{0,1:T(8,128)(2,1)}, u32[]{:S(2)}) copy-start(bf16[1024,832]{0,1:T(8,128)(2,1)} %param.4) | copy-start | bytes 5111812
  49.0 7.2 %copy-start.2 = (f32[32,32,128]{2,1,0:T(8,128)}, f32[32,32,128]{2,1,0:T(8,128)S(1)}, u32[]{:S(2)}) copy-start(f32[32,32,128]{2,1,0:T(8,128)S(1)} %all_to_all.22) | copy-start | bytes 1572868
  49.9 6.8 %collective-permute-start = (f32[544,128]{1,0:T(8,128)S(1)}, f32[544,128]{1,0:T(8,128)S(1)}, u32[]{:S(2)}, u32[]{:S(2)}) collective-permute-start(f32[544,128]{1,0:T(8,128)S(1)} %get-tuple-element.10.give_ref), channel_id=1, source_target_pairs={{0,32},{32,0},{1,33},{33,1},{2,34},{34,2},{3,35},{35,3},{4,36},{36... | collective-permute-start | bytes 835592 | tf_op jit(solution)/shard_map/ppermute | solution.py:331
  56.8 4.5 %collective-permute-start.1 = (f32[128,128]{1,0:T(8,128)S(1)}, f32[128,128]{1,0:T(8,128)S(1)}, u32[]{:S(2)}, u32[]{:S(2)}) collective-permute-start(f32[128,128]{1,0:T(8,128)S(1)} %slice.8), channel_id=1, source_target_pairs={{0,64},{32,224},{64,0},{96,160},{128,192},{160,96},{192,128},{224,... | collective-permute-start | bytes 196616 | tf_op jit(solution)/shard_map/ppermute | solution.py:336
  59.6 6.0 %collective-permute-start.3 = (f32[416,128]{1,0:T(8,128)S(1)}, f32[416,128]{1,0:T(8,128)S(1)}, u32[]{:S(2)}, u32[]{:S(2)}) collective-permute-start(f32[416,128]{1,0:T(8,128)S(1)} %slice.9), channel_id=1, source_target_pairs={{0,64},{32,224},{64,0},{96,160},{128,192},{160,96},{192,128},{224,... | collective-permute-start | bytes 638984 | tf_op jit(solution)/shard_map/ppermute | solution.py:336
  61.3 4.5 %collective-permute-start.2 = (f32[128,128]{1,0:T(8,128)S(1)}, f32[128,128]{1,0:T(8,128)S(1)}, u32[]{:S(2)}, u32[]{:S(2)}) collective-permute-start(f32[128,128]{1,0:T(8,128)S(1)} %slice_add_fusion.gram_ref), channel_id=1, source_target_pairs={{0,192},{32,96},{64,128},{96,32},{128,64},{160,224},{192,0},{224,1... | collective-permute-start | bytes 196616 | tf_op jit(solution)/shard_map/ppermute | solution.py:336
  65.7 13.7 %copy-start.3 = (f32[32,32,128]{2,1,0:T(8,128)S(1)}, f32[32,32,128]{2,1,0:T(8,128)}, u32[]{:S(2)}) copy-start(f32[32,32,128]{2,1,0:T(8,128)} %copy-done.2) | copy-start | bytes 1572868
  65.7 5.1 %collective-permute-start.4 = (f32[416,128]{1,0:T(8,128)S(1)}, f32[416,128]{1,0:T(8,128)S(1)}, u32[]{:S(2)}, u32[]{:S(2)}) collective-permute-start(f32[416,128]{1,0:T(8,128)S(1)} %slice_add_fusion.1.part_ref), channel_id=1, source_target_pairs={{0,192},{32,96},{64,128},{96,32},{128,64},{160,224},{192,0},{224,1... | collective-permute-start | bytes 638984 | tf_op jit(solution)/shard_map/ppermute | solution.py:336
  71.7 7.6 %collective-permute-start.5 = (f32[416,128]{1,0:T(8,128)S(1)}, f32[416,128]{1,0:T(8,128)S(1)}, u32[]{:S(2)}, u32[]{:S(2)}) collective-permute-start(f32[416,128]{1,0:T(8,128)S(1)} %get-tuple-element.11.mine_ref), channel_id=1, source_target_pairs={{0,32},{32,0},{1,33},{33,1},{2,34},{34,2},{3,35},{35,3},{4,36},{36... | collective-permute-start | bytes 638984 | tf_op jit(solution)/shard_map/ppermute | solution.py:331
  73.2 15.2 %all-to-all-start.3 = ((f32[64,1,128]{2,1,0:T(1,128)}), f32[64,1,128]{2,1,0:T(1,128)S(1)}, u32[]{:S(2)}, u32[]{:S(2)}) async-start(f32[64,1,128]{2,1,0:T(1,128)} %bitcast.8), calls=%async_computation.3 | async-start | bytes 65536 | tf_op jit(solution)/shard_map/all_to_all | solution.py:327

commit v7 on v6

--- a/solution.py
+++ b/solution.py
@@ -292,7 +292,7 @@
             pltpu.SemaphoreType.DMA((len(EVEN),)),
         ],
         compiler_params=params(14),
-        cost_estimate=pl.CostEstimate(flops=4 * R * C * RANK, bytes_accessed=R * C * 10, transcendentals=0),
+        cost_estimate=pl.CostEstimate(flops=1 << 20, bytes_accessed=1 << 16, transcendentals=0),
         name="new_momentum",
     )(core, *far(m, g), left, *near(inverse, mine, other))
 

time: 90.5 us -> 90.5 us (level)
  no operation moved by 1% of the time
where the time goes in v7:
time: 90.5 us; the launch traced here: 90.2 us
  blocking collectives  44.4 us (49%)
  starting transfers between devices  16.4 us (18%)
  Pallas kernels  15.9 us (18%)
  waiting for transfers between devices  12.7 us (14%)
    all_to_all x3, blocking collectives, exchange(): return lax.all_to_all(blocks, axes, 0, 0)  44.4 us
    ppermute x2, starting transfers between devices, swap_core(): return lax.ppermute(block, 'core', [(0, 1), (1, 0)])  7.11 us
    ppermute x4, waiting for transfers between devices, swap_y(): return lax.ppermute(block, ('y', 'core'), pairs)  6.91 us
    all_to_all x1, starting transfers between devices, exchange(): return lax.all_to_all(blocks, axes, 0, 0)  6.11 us
    all_to_all x1, waiting for transfers between devices, exchange(): return lax.all_to_all(blocks, axes, 0, 0)  5.28 us
    pallas_call x1, Pallas kernels, left_of(): pl.pallas_call(left_kernel, in_specs=[SMEM, ANY, ANY, ANY], out_specs=WHO...  3.88 us
    pallas_call x1, Pallas kernels, inverse_of(): pl.pallas_call(inverse_kernel, out_shape=pltpu.VMEM((RANK, RANK), F32), i...  3.8 us
    pallas_call x1, Pallas kernels, momentum_of(): pl.pallas_call(momentum_kernel, in_specs=[SMEM, ANY, ANY, ANY, WHOLE, WHO...  3.75 us
  transfers between devices with their start and end apart: 7, of which 5 were waited for; matrix products, arithmetic and copies ran while one was open for 0% of the time, Pallas kernels for 9%

profile of v7, /device:TPU:1, one launch (start us, length us, event | category | flops | bytes accessed | tf_op | source)
XLA Modules:
  0.0 90.2 jit_solution(16524432064530914566)
XLA Ops:
  0.6 0.0 copy-start
  0.7 3.9 %left_part.1 = f32[1024,128]{1,0:T(8,128)S(1)} custom-call(s32[1]{0:T(128)} %bitcast.core_ref, f32[832,1024]{1,0:T(8,128)} %bitcast.12, bf16[832,1024]{1,0:T(8,128)(2,1)} %bitcast.16, f32[832,128]{1,0:T(8,128)} %r_hbm.1), custom_call_target="tpu_custom_call" | custom-call | flops 654311424 | bytes 5111808 | tf_op jit(solution)/shard_map/left_part/pallas_call | solution.py:83
  4.5 13.2 %all_to_all.20.parts_ref = f32[4,256,128]{2,1,0:T(8,128)S(1)} all-to-all(f32[4,256,128]{2,1,0:T(8,128)S(1)} %bitcast.22), channel_id=1, replica_groups=mesh['y'=4,'core'=2,'x'=4,'z'=8] {'x'}, dimensions={0} | all-to-all | bytes 1048576 | tf_op jit(solution)/shard_map/all_to_all | solution.py:327
  17.7 16.1 %all_to_all.21.parts_ref = f32[8,32,128]{2,1,0:T(8,128)S(1)} all-to-all(f32[8,32,128]{2,1,0:T(8,128)S(1)} %bitcast.23), channel_id=1, replica_groups=mesh['y'=4,'core'=2,'x'=4,'z'=8] {'z'}, dimensions={0} | all-to-all | bytes 262144 | tf_op jit(solution)/shard_map/all_to_all | solution.py:327
  33.8 0.1 sum_and_spread.3
  33.9 15.1 %all_to_all.22 = f32[32,32,128]{2,1,0:T(8,128)S(1)} all-to-all(f32[32,32,128]{2,1,0:T(8,128)S(1)} %sum_and_spread.3), channel_id=1, replica_groups=mesh['y'=4,'core'=2,'x'=4,'z'=8] {'x','z'}, dimensions={0} | all-to-all | bytes 1048576 | tf_op jit(solution)/shard_map/all_to_all | solution.py:327
  49.0 0.9 %weighted_give.1 = (f32[544,128]{1,0:T(8,128)S(1)}, bf16[1024,256]{1,0:T(8,128)(2,1)S(1)}) custom-call(s32[1]{0:T(128)} %bitcast.core_ref, f32[1024,128]{1,0:T(8,128)S(1)} %bitcast.20, f32[832,1024]{1,0:T(8,128)S(1)} %bitcast.14, bf16[832,1024]{1,0:T(8,128)(2,1)S(1)} %bitcast.18), custom_call_target="tpu_custom_call" | custom-call | flops 327155712 | bytes 2555904 | tf_op jit(solution)/shard_map/weighted_give/pallas_call | solution.py:148
  49.9 5.6 %collective-permute-start = (f32[544,128]{1,0:T(8,128)S(1)}, f32[544,128]{1,0:T(8,128)S(1)}, u32[]{:S(2)}, u32[]{:S(2)}) collective-permute-start(f32[544,128]{1,0:T(8,128)S(1)} %get-tuple-element.10.give_ref), channel_id=1, source_target_pairs={{0,32},{32,0},{1,33},{33,1},{2,34},{34,2},{3,35},{35,3},{4,36},{36... | collective-permute-start | bytes 835592 | tf_op jit(solution)/shard_map/ppermute | solution.py:331
  55.6 0.6 weighted_keep.1
  56.2 0.5 collective-permute-done
  56.8 2.8 %collective-permute-start.1 = (f32[128,128]{1,0:T(8,128)S(1)}, f32[128,128]{1,0:T(8,128)S(1)}, u32[]{:S(2)}, u32[]{:S(2)}) collective-permute-start(f32[128,128]{1,0:T(8,128)S(1)} %slice.8), channel_id=1, source_target_pairs={{0,64},{32,224},{64,0},{96,160},{128,192},{160,96},{192,128},{224,... | collective-permute-start | bytes 196616 | tf_op jit(solution)/shard_map/ppermute | solution.py:336
  59.6 0.1 collective-permute-start.3
  59.7 1.5 %collective-permute-done.1 = f32[128,128]{1,0:T(8,128)S(1)} collective-permute-done((f32[128,128]{1,0:T(8,128)S(1)}, f32[128,128]{1,0:T(8,128)S(1)}, u32[]{:S(2)}, u32[]{:S(2)}) %collective-permute-start.1) | collective-permute-done | bytes 65568 | tf_op jit(solution)/shard_map/ppermute | solution.py:336
  61.3 0.1 collective-permute-start.2
  61.4 4.2 %collective-permute-done.3 = f32[416,128]{1,0:T(8,128)S(1)} collective-permute-done((f32[416,128]{1,0:T(8,128)S(1)}, f32[416,128]{1,0:T(8,128)S(1)}, u32[]{:S(2)}, u32[]{:S(2)}) %collective-permute-start.3) | collective-permute-done | bytes 213024 | tf_op jit(solution)/shard_map/ppermute | solution.py:336
  65.7 0.1 collective-permute-start.4
  65.8 3.8 %inverse_factor.1.inverse_ref = f32[128,128]{1,0:T(8,128)S(1)} custom-call(f32[128,128]{1,0:T(8,128)S(1)} %slice_add_fusion.gram_ref, f32[128,128]{1,0:T(8,128)S(1)} %collective-permute-done.2.got_ref), custom_call_target="tpu_custom_call" | custom-call | flops 64424509440 | bytes 131072 | tf_op jit(solution)/shard_map/inverse_factor/pallas_call | solution.py:209
  69.6 1.2 %collective-permute-done.4.got_ref = f32[416,128]{1,0:T(8,128)S(1)} collective-permute-done((f32[416,128]{1,0:T(8,128)S(1)}, f32[416,128]{1,0:T(8,128)S(1)}, u32[]{:S(2)}, u32[]{:S(2)}) %collective-permute-start.4) | collective-permute-done | bytes 213024 | tf_op jit(solution)/shard_map/ppermute | solution.py:336
  70.7 1.0 %across_part.1 = (f32[416,128]{1,0:T(8,128)S(1)}, f32[64,128]{1,0:T(8,128)}) custom-call(f32[416,128]{1,0:T(8,128)S(1)} %slice_add_fusion.1.part_ref, f32[416,128]{1,0:T(8,128)S(1)} %collective-permute-done.4.got_ref, f32[128,128]{1,0:T(8,128)S(1)} %inverse_factor.1.inverse_ref), custom_call_target="tpu_custom_call" | custom-call | flops 81788928 | bytes 851968 | tf_op jit(solution)/shard_map/across_part/pallas_call | solution.py:231
  71.7 1.5 %collective-permute-start.5 = (f32[416,128]{1,0:T(8,128)S(1)}, f32[416,128]{1,0:T(8,128)S(1)}, u32[]{:S(2)}, u32[]{:S(2)}) collective-permute-start(f32[416,128]{1,0:T(8,128)S(1)} %get-tuple-element.11.mine_ref), channel_id=1, source_target_pairs={{0,32},{32,0},{1,33},{33,1},{2,34},{34,2},{3,35},{35,3},{4,36},{36... | collective-permute-start | bytes 638984 | tf_op jit(solution)/shard_map/ppermute | solution.py:331
  73.2 6.1 %all-to-all-start.3 = ((f32[64,1,128]{2,1,0:T(1,128)}), f32[64,1,128]{2,1,0:T(1,128)S(1)}, u32[]{:S(2)}, u32[]{:S(2)}) async-start(f32[64,1,128]{2,1,0:T(1,128)} %bitcast.8), calls=%async_computation.3 | async-start | bytes 65536 | tf_op jit(solution)/shard_map/all_to_all | solution.py:327
  79.3 3.7 %new_momentum.1 = (f32[832,1024]{1,0:T(8,128)}, bf16[384,1024]{1,0:T(8,128)(2,1)S(1)}, f32[832,128]{1,0:T(8,128)S(1)}) custom-call(s32[1]{0:T(128)} %bitcast.core_ref, f32[832,1024]{1,0:T(8,128)} %bitcast.13, bf16[832,1024]{1,0:T(8,128)(2,1)} %bitcast.17, f32[1024,128]{1,0:T(8,128)S(1)} %bitcast.21, f32[128,128]{1,0:T(8,128)S(1)} %inverse_factor.1.inverse_ref, ...), custom_call_target="tpu_custom_call" | custom-call | flops 1048576 | bytes 65536 | tf_op jit(solution)/shard_map/new_momentum/pallas_call | solution.py:280
  83.1 5.3 %all-to-all-done.3 = f32[64,1,128]{2,1,0:T(1,128)S(1)} async-done(((f32[64,1,128]{2,1,0:T(1,128)}), f32[64,1,128]{2,1,0:T(1,128)S(1)}, u32[]{:S(2)}, u32[]{:S(2)}) %all-to-all-start.3) | async-done | bytes 32800 | tf_op jit(solution)/shard_map/all_to_all | solution.py:327
  88.4 1.9 %update.1 = bf16[832,1024]{1,0:T(8,128)(2,1)} custom-call(f32[832,128]{1,0:T(8,128)S(1)} %get-tuple-element.13.across_ref, f32[64,128]{1,0:T(8,128)S(1)} %bitcast.24, bf16[384,1024]{1,0:T(8,128)(2,1)S(1)} %get-tuple-element.15.basis_ref), custom_call_target="tpu_custom_call" | custom-call | flops 654311424 | bytes 1703936 | tf_op jit(solution)/shard_map/update/pallas_call | solution.py:314
  (15 shorter events, 0.1 us)
Async XLA Ops:
  0.6 48.4 %copy-start = (f32[1024,832]{0,1:T(8,128)S(1)}, f32[1024,832]{0,1:T(8,128)}, u32[]{:S(2)}) copy-start(f32[1024,832]{0,1:T(8,128)} %param.3) | copy-start | bytes 10223620
  0.6 48.4 %copy-start.1 = (bf16[1024,832]{0,1:T(8,128)(2,1)S(1)}, bf16[1024,832]{0,1:T(8,128)(2,1)}, u32[]{:S(2)}) copy-start(bf16[1024,832]{0,1:T(8,128)(2,1)} %param.4) | copy-start | bytes 5111812
  49.0 7.2 %copy-start.2 = (f32[32,32,128]{2,1,0:T(8,128)}, f32[32,32,128]{2,1,0:T(8,128)S(1)}, u32[]{:S(2)}) copy-start(f32[32,32,128]{2,1,0:T(8,128)S(1)} %all_to_all.22) | copy-start | bytes 1572868
  49.9 6.8 %collective-permute-start = (f32[544,128]{1,0:T(8,128)S(1)}, f32[544,128]{1,0:T(8,128)S(1)}, u32[]{:S(2)}, u32[]{:S(2)}) collective-permute-start(f32[544,128]{1,0:T(8,128)S(1)} %get-tuple-element.10.give_ref), channel_id=1, source_target_pairs={{0,32},{32,0},{1,33},{33,1},{2,34},{34,2},{3,35},{35,3},{4,36},{36... | collective-permute-start | bytes 835592 | tf_op jit(solution)/shard_map/ppermute | solution.py:331
  56.8 4.5 %collective-permute-start.1 = (f32[128,128]{1,0:T(8,128)S(1)}, f32[128,128]{1,0:T(8,128)S(1)}, u32[]{:S(2)}, u32[]{:S(2)}) collective-permute-start(f32[128,128]{1,0:T(8,128)S(1)} %slice.8), channel_id=1, source_target_pairs={{0,64},{32,224},{64,0},{96,160},{128,192},{160,96},{192,128},{224,... | collective-permute-start | bytes 196616 | tf_op jit(solution)/shard_map/ppermute | solution.py:336
  59.6 6.0 %collective-permute-start.3 = (f32[416,128]{1,0:T(8,128)S(1)}, f32[416,128]{1,0:T(8,128)S(1)}, u32[]{:S(2)}, u32[]{:S(2)}) collective-permute-start(f32[416,128]{1,0:T(8,128)S(1)} %slice.9), channel_id=1, source_target_pairs={{0,64},{32,224},{64,0},{96,160},{128,192},{160,96},{192,128},{224,... | collective-permute-start | bytes 638984 | tf_op jit(solution)/shard_map/ppermute | solution.py:336
  61.3 4.5 %collective-permute-start.2 = (f32[128,128]{1,0:T(8,128)S(1)}, f32[128,128]{1,0:T(8,128)S(1)}, u32[]{:S(2)}, u32[]{:S(2)}) collective-permute-start(f32[128,128]{1,0:T(8,128)S(1)} %slice_add_fusion.gram_ref), channel_id=1, source_target_pairs={{0,192},{32,96},{64,128},{96,32},{128,64},{160,224},{192,0},{224,1... | collective-permute-start | bytes 196616 | tf_op jit(solution)/shard_map/ppermute | solution.py:336
  65.7 13.7 %copy-start.3 = (f32[32,32,128]{2,1,0:T(8,128)S(1)}, f32[32,32,128]{2,1,0:T(8,128)}, u32[]{:S(2)}) copy-start(f32[32,32,128]{2,1,0:T(8,128)} %copy-done.2) | copy-start | bytes 1572868
  65.7 5.1 %collective-permute-start.4 = (f32[416,128]{1,0:T(8,128)S(1)}, f32[416,128]{1,0:T(8,128)S(1)}, u32[]{:S(2)}, u32[]{:S(2)}) collective-permute-start(f32[416,128]{1,0:T(8,128)S(1)} %slice_add_fusion.1.part_ref), channel_id=1, source_target_pairs={{0,192},{32,96},{64,128},{96,32},{128,64},{160,224},{192,0},{224,1... | collective-permute-start | bytes 638984 | tf_op jit(solution)/shard_map/ppermute | solution.py:336
  71.7 7.6 %collective-permute-start.5 = (f32[416,128]{1,0:T(8,128)S(1)}, f32[416,128]{1,0:T(8,128)S(1)}, u32[]{:S(2)}, u32[]{:S(2)}) collective-permute-start(f32[416,128]{1,0:T(8,128)S(1)} %get-tuple-element.11.mine_ref), channel_id=1, source_target_pairs={{0,32},{32,0},{1,33},{33,1},{2,34},{34,2},{3,35},{35,3},{4,36},{36... | collective-permute-start | bytes 638984 | tf_op jit(solution)/shard_map/ppermute | solution.py:331
  73.2 15.2 %all-to-all-start.3 = ((f32[64,1,128]{2,1,0:T(1,128)}), f32[64,1,128]{2,1,0:T(1,128)S(1)}, u32[]{:S(2)}, u32[]{:S(2)}) async-start(f32[64,1,128]{2,1,0:T(1,128)} %bitcast.8), calls=%async_computation.3 | async-start | bytes 65536 | tf_op jit(solution)/shard_map/all_to_all | solution.py:327
